TPU v7x, 32 devices: a whole 2x2x4 slice. The times are simulated.
32 devices in a mesh: canvas: 4 (over y, x), height: 8 (over z, core).
Axes of the slice: x: 2, y: 2, z: 4, core: 2. Of those that a mesh axis runs over, the one named last changes fastest.
Arguments:
- features: bfloat16 [4, 64, 16, 512], P('canvas', 'height')
- tile_ids: int32 [4, 64], P('canvas'), may hold values from 0 to 63, as said below
- norm_gains: float32 [3, 512], replicated, may hold values from 0.5 to 1.5
- norm_shifts: float32 [3, 512], replicated, may hold values from -1.5 to 1.5
- conv_weights: bfloat16 [2, 3, 3, 512, 512], replicated, may hold values from -0.09375 to 0.09375
- conv_biases: float32 [2, 512], replicated, may hold values from -1.5 to 1.5
- qkv_weight: bfloat16 [512, 1536], replicated, may hold values from -0.25 to 0.25
- qv_bias: float32 [2, 512], replicated, may hold values from -2.5 to 2.5
- proj_weight: bfloat16 [512, 512], replicated, may hold values from -2 to 2
- proj_bias: float32 [512], replicated, may hold values from -1.5 to 1.5
- cotangent: bfloat16 [4, 64, 16, 512], P('canvas', 'height'), may hold values from -6 to 6
Outputs:
- output: bfloat16 [4, 64, 16, 512], P('canvas', 'height')
- input_grad: bfloat16 [4, 64, 16, 512], P('canvas', 'height')
- norm_gains_grad: float32 [3, 512], replicated
- norm_shifts_grad: float32 [3, 512], replicated
- conv_weights_grad: float32 [2, 3, 3, 512, 512], P(None, None, None, 'canvas', 'height')
- conv_biases_grad: float32 [2, 512], replicated
- qkv_weight_grad: float32 [512, 1536], replicated
- qv_bias_grad: float32 [2, 512], replicated
- proj_weight_grad: float32 [512, 512], replicated
- proj_bias_grad: float32 [512], replicated
Inputs may be any that keep to these rules, and one draw needn't show every extreme that they name: `tile_ids`: within each canvas a row's id is the index of the first row of its latent image, so ids start at 0 and never fall; rows that share an id form one latent image of 16 columns. One canvas holds a single image over all its rows; in every other canvas the last row begins an image of its own.
All inputs are finite; a program needn't handle non-finite values.
Results may differ from a plain program's by a relative error of at most 0.014.
Values may be sent and summed in bfloat16 or wider, within the bound.
No kernel may reach another device: no remote copies, remote signals or barrier semaphores. Data moves between devices by JAX's collectives and lax.ppermute only.
A program may use at most 256 MiB of HBM per device.

v0:
```python
import functools

import jax
import jax.numpy as jnp
from jax import lax
from jax.experimental import pallas as pl
from jax.experimental.pallas import tpu as pltpu
from jax.sharding import PartitionSpec as P

GROUPS = 32


epsilon = 1e-06
masked_score = -1e30
MOST_PIXELS = 1024
LANES = 128
NARROW = 128
CHUNK = 128
FILL_ROWS = 256
QUERY_ROWS = 512
SCORE_ROWS = 256
KEY_ROWS = 512


def extended(block, sides, width):
    for axis, dim in sides:
        count = lax.axis_size(axis)
        forward = [(i, i + 1) for i in range(count - 1)]
        backward = [(target, source) for source, target in forward]
        low = lax.ppermute(
            lax.slice_in_dim(block, block.shape[dim] - width, None, axis=dim), axis, forward
        )
        high = lax.ppermute(lax.slice_in_dim(block, 0, width, axis=dim), axis, backward)
        block = jnp.concatenate([low, block, high], axis=dim)
    return block


def group_total(vector):
    return vector.reshape(GROUPS, -1).sum(axis=1)


def spread_groups(vector, channels):
    return jnp.repeat(vector, channels // GROUPS)


def norm_forward(values, gain, shift, members):
    channels = values.shape[1]
    totals = lax.psum(group_total(jnp.sum(values, axis=0)), "height")
    centered = values - spread_groups(totals / members, channels)
    squares = lax.psum(group_total(jnp.sum(centered * centered, axis=0)), "height")
    inverse = spread_groups(lax.rsqrt(squares / members + epsilon), channels)
    normed = centered * inverse
    return (normed, inverse, normed * gain + shift)


def norm_backward(grad_in, normed, inverse, gain, members):
    channels = grad_in.shape[1]
    scaled = grad_in * gain
    both_sums = lax.psum(
        (group_total(jnp.sum(scaled, axis=0)), group_total(jnp.sum(scaled * normed, axis=0))),
        "height",
    )
    mean_grad = spread_groups(both_sums[0] / members, channels)
    mean_cross = spread_groups(both_sums[1] / members, channels)
    result = inverse * (scaled - mean_grad - normed * mean_cross)
    return (result, jnp.sum(grad_in * normed, axis=0), jnp.sum(grad_in, axis=0))


def swish(values):
    return values * jax.nn.sigmoid(values)


def swish_slope(values):
    sigmoid_part = jax.nn.sigmoid(values)
    return sigmoid_part * (1.0 + values * (1.0 - sigmoid_part))


def tap_columns(padded, row_mask, local_rows, canvas_cols):
    pieces = []
    for row_tap in range(3):
        rows_taken = padded[row_tap : row_tap + local_rows] * row_mask[:, row_tap, None, None]
        for col_tap in range(3):
            pieces.append(rows_taken[:, col_tap : col_tap + canvas_cols])
    stacked = jnp.concatenate(pieces, axis=2)
    return stacked.reshape(local_rows * canvas_cols, stacked.shape[2])


def conv_forward(acts, row_mask, weight, bias):
    local_rows, canvas_cols, channels = acts.shape
    rimmed = extended(acts, (("height", 0),), 1)
    padded = jnp.pad(rimmed, ((0, 0), (1, 1), (0, 0)))
    gathered = tap_columns(padded, row_mask, local_rows, canvas_cols)
    result = (
        jnp.dot(
            gathered, weight.reshape(9 * channels, channels), preferred_element_type=jnp.float32
        )
        + bias
    )
    return (result, gathered)


def conv_backward(grad_low, row_mask, weight, gathered):
    local_rows, canvas_cols, channels = grad_low.shape
    flat_grad = grad_low.reshape(local_rows * canvas_cols, channels)
    weight_grad = lax.dot_general(
        gathered, flat_grad, (((0,), (0,)), ((), ())), preferred_element_type=jnp.float32
    )
    rimmed = extended(grad_low, (("height", 0),), 1)
    padded = jnp.pad(rimmed, ((0, 0), (1, 1), (0, 0)))
    grad_taps = tap_columns(padded, row_mask, local_rows, canvas_cols)
    flipped = jnp.transpose(weight[::-1, ::-1], (0, 1, 3, 2)).reshape(9 * channels, channels)
    input_part = jnp.dot(grad_taps, flipped, preferred_element_type=jnp.float32)
    return (
        input_part,
        weight_grad.reshape(3, 3, channels, channels),
        jnp.sum(flat_grad.astype(jnp.float32), axis=0),
    )


def take_rows(array, offset, count):
    return lax.dynamic_slice_in_dim(array, offset, count)


def score_grads(
    queries, out_grad, log_total, row_dots, query_ids, key_rows, value_rows, key_ids, score_scale
):
    scores = (
        lax.dot_general(
            queries, key_rows, (((1,), (1,)), ((), ())), preferred_element_type=jnp.float32
        )
        * score_scale
    )
    same_tile = query_ids[:, None] == key_ids[None, :]
    softmax_block = jnp.exp(jnp.where(same_tile, scores - log_total[:, None], masked_score))
    weight_grad = lax.dot_general(
        out_grad, value_rows, (((1,), (1,)), ((), ())), preferred_element_type=jnp.float32
    )
    score_grad = (softmax_block * (weight_grad - row_dots[:, None])).astype(jnp.bfloat16)
    return (softmax_block.astype(jnp.bfloat16), score_grad)


def split_canvas(
    features,
    tile_ids,
    norm_gains,
    norm_shifts,
    conv_weights,
    conv_biases,
    qkv_weight,
    qv_bias,
    proj_weight,
    proj_bias,
    cotangent,
):
    height_size = lax.axis_size("height")
    local_rows = features.shape[1]
    canvas_cols = features.shape[2]
    channels = features.shape[3]
    pixels = local_rows * canvas_cols
    row_ids = tile_ids[0]
    all_rows = row_ids.shape[0]
    members = float(all_rows * canvas_cols * (channels // GROUPS))
    score_scale = channels ** (-0.5)
    first_row = lax.axis_index("height") * local_rows
    edge_ids = jnp.full((1,), -1, jnp.int32)
    padded_ids = jnp.concatenate([edge_ids, row_ids, edge_ids])
    near_ids = lax.dynamic_slice_in_dim(padded_ids, first_row, local_rows + 2)
    own_rows = near_ids[1 : local_rows + 1]
    row_mask = jnp.stack(
        [near_ids[row_tap : row_tap + local_rows] == own_rows for row_tap in range(3)], axis=1
    ).astype(jnp.bfloat16)
    key_ids = jnp.repeat(row_ids, canvas_cols)
    query_ids = jnp.repeat(own_rows, canvas_cols)
    grid_shape = (local_rows, canvas_cols, channels)
    inputs = features[0].reshape(pixels, channels).astype(jnp.float32)
    normed_one, inverse_one, pre_one = norm_forward(inputs, norm_gains[0], norm_shifts[0], members)
    act_one = swish(pre_one).astype(jnp.bfloat16).reshape(grid_shape)
    middle, taps_one = conv_forward(act_one, row_mask, conv_weights[0], conv_biases[0])
    normed_two, inverse_two, pre_two = norm_forward(middle, norm_gains[1], norm_shifts[1], members)
    act_two = swish(pre_two).astype(jnp.bfloat16).reshape(grid_shape)
    branch, taps_two = conv_forward(act_two, row_mask, conv_weights[1], conv_biases[1])
    residual = inputs + branch
    normed_three, inverse_three, pre_three = norm_forward(
        residual, norm_gains[2], norm_shifts[2], members
    )
    attn_input = pre_three.astype(jnp.bfloat16)
    mixed = jnp.dot(attn_input, qkv_weight, preferred_element_type=jnp.float32)
    queries = (mixed[:, :channels] + qv_bias[0]).astype(jnp.bfloat16)
    key_rows = mixed[:, channels : 2 * channels].astype(jnp.bfloat16)
    value_rows = (mixed[:, 2 * channels :] + qv_bias[1]).astype(jnp.bfloat16)
    running_max = jnp.full((pixels,), masked_score, jnp.float32)
    key_piece = lax.all_gather(key_rows, "height", axis=0, tiled=True)
    value_piece = lax.all_gather(value_rows, "height", axis=0, tiled=True)
    scores = (
        lax.dot_general(
            queries, key_piece, (((1,), (1,)), ((), ())), preferred_element_type=jnp.float32
        )
        * score_scale
    )
    same_tile = query_ids[:, None] == key_ids[None, :]
    scores = jnp.where(same_tile, scores, masked_score)
    new_max = jnp.maximum(running_max, jnp.max(scores, axis=1))
    weights = jnp.where(same_tile, jnp.exp(scores - new_max[:, None]), 0.0)
    summed_out = jnp.dot(
        weights.astype(jnp.bfloat16), value_piece, preferred_element_type=jnp.float32
    )
    total_weight = jnp.sum(weights, axis=1)
    log_total = new_max + jnp.log(total_weight)
    attended = summed_out / total_weight[:, None]
    attended_low = attended.astype(jnp.bfloat16)
    output = (
        residual
        + jnp.dot(attended_low, proj_weight, preferred_element_type=jnp.float32)
        + proj_bias
    )
    out_grad = cotangent[0].reshape(pixels, channels)
    out_grad_full = out_grad.astype(jnp.float32)
    proj_grad = lax.dot_general(
        attended_low, out_grad, (((0,), (0,)), ((), ())), preferred_element_type=jnp.float32
    )
    proj_bias_grad = jnp.sum(out_grad_full, axis=0)
    attended_grad = lax.dot_general(
        out_grad, proj_weight, (((1,), (1,)), ((), ())), preferred_element_type=jnp.float32
    ).astype(jnp.bfloat16)
    row_dots = jnp.sum(attended_grad.astype(jnp.float32) * attended, axis=1)
    block_rows = pixels * min(height_size, 8)
    zero_block = jnp.zeros((pixels, channels), jnp.float32)
    key_all, value_all = (
        lax.all_gather(key_rows, "height", axis=0, tiled=True),
        lax.all_gather(value_rows, "height", axis=0, tiled=True),
    )
    query_all, grad_all = (
        lax.all_gather(queries, "height", axis=0, tiled=True),
        lax.all_gather(attended_grad, "height", axis=0, tiled=True),
    )
    total_all, dots_all = (
        lax.all_gather(log_total, "height", axis=0, tiled=True),
        lax.all_gather(row_dots, "height", axis=0, tiled=True),
    )

    def own_query_step(running, block_index):
        offset = block_index * block_rows
        key_part = take_rows(key_all, offset, block_rows)
        rounded, score_grad = score_grads(
            queries,
            attended_grad,
            log_total,
            row_dots,
            query_ids,
            key_part,
            take_rows(value_all, offset, block_rows),
            take_rows(key_ids, offset, block_rows),
            score_scale,
        )
        return (
            running
            + jnp.dot(score_grad, key_part, preferred_element_type=jnp.float32) * score_scale,
            None,
        )

    def own_key_step(running, block_index):
        offset = block_index * block_rows
        query_part = take_rows(query_all, offset, block_rows)
        grad_part = take_rows(grad_all, offset, block_rows)
        rounded, score_grad = score_grads(
            query_part,
            grad_part,
            take_rows(total_all, offset, block_rows),
            take_rows(dots_all, offset, block_rows),
            take_rows(key_ids, offset, block_rows),
            key_rows,
            value_rows,
            query_ids,
            score_scale,
        )
        key_part = (
            lax.dot_general(
                score_grad, query_part, (((0,), (0,)), ((), ())), preferred_element_type=jnp.float32
            )
            * score_scale
        )
        value_part = lax.dot_general(
            rounded, grad_part, (((0,), (0,)), ((), ())), preferred_element_type=jnp.float32
        )
        return ((running[0] + key_part, running[1] + value_part), None)

    block_count = key_all.shape[0] // block_rows
    query_grad, unused_one = lax.scan(own_query_step, zero_block, jnp.arange(block_count))
    (key_grad, value_grad), unused_two = lax.scan(
        own_key_step, (zero_block, zero_block), jnp.arange(block_count)
    )
    query_low = query_grad.astype(jnp.bfloat16)
    key_low = key_grad.astype(jnp.bfloat16)
    value_low = value_grad.astype(jnp.bfloat16)
    stacked_grad = jnp.concatenate([query_low, key_low, value_low], axis=1)
    qkv_grad = lax.dot_general(
        attn_input, stacked_grad, (((0,), (0,)), ((), ())), preferred_element_type=jnp.float32
    )
    qv_grad = jnp.stack(
        [
            jnp.sum(query_low.astype(jnp.float32), axis=0),
            jnp.sum(value_low.astype(jnp.float32), axis=0),
        ]
    )
    normed_grad = lax.dot_general(
        stacked_grad, qkv_weight, (((1,), (1,)), ((), ())), preferred_element_type=jnp.float32
    )
    back_three, gain_three, shift_three = norm_backward(
        normed_grad, normed_three, inverse_three, norm_gains[2], members
    )
    residual_grad = out_grad_full + back_three
    grad_two = residual_grad.astype(jnp.bfloat16).reshape(grid_shape)
    act_two_grad, weight_two_grad, bias_two_grad = conv_backward(
        grad_two, row_mask, conv_weights[1], taps_two
    )
    middle_grad, gain_two, shift_two = norm_backward(
        act_two_grad * swish_slope(pre_two), normed_two, inverse_two, norm_gains[1], members
    )
    grad_one = middle_grad.astype(jnp.bfloat16).reshape(grid_shape)
    act_one_grad, weight_one_grad, bias_one_grad = conv_backward(
        grad_one, row_mask, conv_weights[0], taps_one
    )
    input_back, gain_one, shift_one = norm_backward(
        act_one_grad * swish_slope(pre_one), normed_one, inverse_one, norm_gains[0], members
    )
    input_grad = residual_grad + input_back
    conv_grad = jnp.stack([weight_one_grad, weight_two_grad])
    conv_part = lax.psum_scatter(conv_grad, "height", scatter_dimension=4, tiled=True)
    conv_part = lax.psum_scatter(
        conv_part.astype(jnp.bfloat16), "canvas", scatter_dimension=3, tiled=True
    ).astype(jnp.float32)
    summed = lax.psum(
        (
            jnp.stack([gain_one, gain_two, gain_three]),
            jnp.stack([shift_one, shift_two, shift_three]),
            jnp.stack([bias_one_grad, bias_two_grad]),
            qkv_grad,
            qv_grad,
            proj_grad,
            proj_bias_grad,
        ),
        ("canvas", "height"),
    )
    return (
        output.astype(jnp.bfloat16).reshape((1,) + grid_shape),
        input_grad.astype(jnp.bfloat16).reshape((1,) + grid_shape),
        summed[0],
        summed[1],
        conv_part,
        summed[2],
        summed[3],
        summed[4],
        summed[5],
        summed[6],
    )


def fold(block):
    rows, width = block.shape
    return jnp.sum(block.reshape(rows // 8, 8, width), axis=0)


def group_lanes(block, group):
    lane = lax.broadcasted_iota(jnp.int32, block.shape, 1)
    width = block.shape[1]
    step = 1
    while step < group:
        above = pltpu.roll(block, step, 1)
        below = pltpu.roll(block, width - step, 1)
        block = block + jnp.where((lane & step) != 0, above, below)
        step *= 2
    return block


def group_mean(partial, members):
    spread = group_lanes(partial, partial.shape[1] // GROUPS)
    return jnp.sum(spread, axis=0, keepdims=True) * (1.0 / members)


def widen(block, width):
    return jnp.concatenate([block] * (width // block.shape[1]), axis=1)


def each_block(pixels, block, body, carry=0):
    def step(index, carry):
        return body(pl.ds(pl.multiple_of(index * block, block), block), carry)

    return lax.fori_loop(0, pixels // block, step, carry)


def each_chunk(pixels, body, carry):
    return each_block(pixels, CHUNK, body, carry)


def aligned(start, step):
    return start if isinstance(start, int) else pl.multiple_of(start, step)


class RunningStats:
    def __init__(self, channels):
        self.width = channels // GROUPS
        self.reference = None
        self.sums = self.squares = jnp.zeros((8, channels), jnp.float32)

    def add(self, block):
        if self.reference is None:
            self.reference = group_mean(block[0:8], 8.0 * self.width)
        offset = block - self.reference
        self.sums = self.sums + fold(offset)
        self.squares = self.squares + fold(offset * offset)

    def finish(self, pixels):
        both = group_lanes(jnp.concatenate([self.sums, self.squares], axis=0), self.width)
        share = 1.0 / (pixels * self.width)
        offset = column_total(both[0:8]) * share
        variance = column_total(both[8:16]) * share - offset * offset
        return self.reference + offset, lax.rsqrt(jnp.maximum(variance, 0.0) + epsilon)


def put_taps(taps_ref, block, rows, cols):
    count, channels = block.shape
    place = lax.broadcasted_iota(jnp.int32, block.shape, 0) & (cols - 1)
    left = jnp.where(place == 0, 0.0, pltpu.roll(block, 1, 0))
    right = jnp.where(place == cols - 1, 0.0, pltpu.roll(block, count - 1, 0))
    inner = pl.ds(aligned(rows.start + cols, cols), count)
    taps_ref[inner, 0:channels] = left.astype(jnp.bfloat16)
    taps_ref[inner, channels : 2 * channels] = block.astype(jnp.bfloat16)
    taps_ref[inner, 2 * channels :] = right.astype(jnp.bfloat16)


def clear_edges(taps_ref, cols):
    edge = jnp.zeros((cols, taps_ref.shape[1]), taps_ref.dtype)
    taps_ref[0:cols, :] = edge
    taps_ref[taps_ref.shape[0] - cols :, :] = edge


def begin_conv(taps_ref, product, total_ref, fill, first, cols):
    for start in range(0, total_ref.shape[0], FILL_ROWS):
        for inner in range(start, start + FILL_ROWS, CHUNK):
            fill(pl.ds(inner, CHUNK))
        rows = pl.ds(start, FILL_ROWS)
        total_ref[rows, :] = first(rows, product(taps_ref, pl.ds(start + cols, FILL_ROWS), 1))


def add_rows(taps_ref, product, mask_ref, total_ref, row_tap, last, cols, old_ref=None):
    pixels, channels = total_ref.shape
    old_ref = total_ref if old_ref is None else old_ref

    def step(rows, shifted):
        part = product(taps_ref, shifted, row_tap)
        mask = widen(mask_ref[row_tap // 2, rows, :], channels)
        value = old_ref[rows, :] + mask * part
        total_ref[rows, :] = value if last is None else last(rows, value)

    block = 2 * FILL_ROWS if last is None else FILL_ROWS
    for start in range(0, pixels, block):
        step(pl.ds(start, block), pl.ds(start + row_tap * cols, block))


def run_conv(taps_ref, product, mask_ref, total_ref, fill, first, last, cols):
    begin_conv(taps_ref, product, total_ref, fill, first, cols)
    add_rows(taps_ref, product, mask_ref, total_ref, 0, None, cols)
    add_rows(taps_ref, product, mask_ref, total_ref, 2, last, cols)


def product_forward(weight_ref):
    channels = weight_ref.shape[-1]

    def product(taps_ref, shifted, row_tap):
        return jnp.dot(
            taps_ref[shifted, :],
            weight_ref[row_tap].reshape(3 * channels, channels),
            preferred_element_type=jnp.float32,
        )

    return product


def product_backward(weight_ref):
    def product(taps_ref, shifted, row_tap):
        return lax.dot_general(
            taps_ref[shifted, :],
            weight_ref[row_tap],
            (((1,), (1,)), ((), ())),
            preferred_element_type=jnp.float32,
        )

    return product


def activation(read, mean, inverse, gain, shift, act_ref, taps_ref, cols):
    scale, offset = 0.5 * inverse * gain, 0.5 * shift

    def fill(rows):
        half = (read(rows) - mean) * scale + offset
        act = half * (1.0 + jnp.tanh(half))
        act_ref[rows, :] = act.astype(jnp.bfloat16)
        put_taps(taps_ref, act, rows, cols)

    return fill


def back_means(sums, gain, pixels):
    channels = gain.shape[1]
    members = float(pixels * (channels // GROUPS))
    return group_mean(sums[0] * gain, members), group_mean(sums[1] * gain, members)


def column_total(partial):
    return jnp.sum(partial, axis=0, keepdims=True)


def weight_part(act_ref, narrow, lanes_ref, flip_ref, columns_ref, part_ref, cols):
    pixels, channels = act_ref.shape
    height = lax.axis_index("height")
    share = NARROW // 2
    flip_ref[...] = narrow.T
    own = pl.ds(pl.multiple_of((height % 2) * share, share), share)
    grad = flip_ref[own, :].astype(jnp.float32)
    column = lax.broadcasted_iota(jnp.int32, grad.shape, 1) & (cols - 1)
    for col_tap in range(3):
        shifted = grad
        if col_tap == 0:
            shifted = jnp.where(column == cols - 1, 0.0, pltpu.roll(grad, pixels - 1, 1))
        elif col_tap == 2:
            shifted = jnp.where(column == 0, 0.0, pltpu.roll(grad, 1, 1))
        for row_tap in range(3):
            tap = 3 * row_tap + col_tap
            place = slice(tap * share, (tap + 1) * share)
            if row_tap == 1:
                columns_ref[place, :] = shifted.astype(jnp.bfloat16)
                continue
            side, turn = (0, pixels - cols) if row_tap == 0 else (1, cols)
            masked = (shifted * lanes_ref[side : side + 1, :]).astype(jnp.bfloat16)
            columns_ref[place, :] = pltpu.roll(masked, turn, 1)
    part_ref[...] = jnp.dot(
        columns_ref[...], act_ref[...], preferred_element_type=jnp.float32
    ).astype(jnp.bfloat16)


def begin_back(grad_ref, weights_ref, mask_ref, taps_ref, total_ref, cols):
    clear_edges(taps_ref, cols)

    def fill(rows):
        put_taps(taps_ref, grad_ref[rows, :].astype(jnp.float32), rows, cols)

    product = product_backward(weights_ref)
    begin_conv(taps_ref, product, total_ref, fill, lambda rows, part: part, cols)
    add_rows(taps_ref, product, mask_ref, total_ref, 0, None, cols)


def finish_back(
    weights_ref, mask_ref, taps_ref, total_ref, read, table_ref, which, cols, old_ref=None
):
    mean, inverse, gain, shift = norm_rows(table_ref, which)
    scale, offset = 0.5 * inverse * gain, 0.5 * shift
    sums = []

    def slope(rows, value):
        centered = read(rows) - mean
        half = centered * scale + offset
        turn = jnp.tanh(half)
        double = value * ((1.0 + turn) * (1.0 + half * (1.0 - turn)))
        sums.append((fold(double), fold(double * centered)))
        return double

    add_rows(
        taps_ref, product_backward(weights_ref), mask_ref, total_ref, 2, slope, cols, old_ref
    )
    plain, cross = sum(pair[0] for pair in sums), sum(pair[1] for pair in sums)
    return 0.5 * plain, 0.5 * inverse * cross


def norm_back(total_ref, double, sums, read, table_ref, which, pixels, scales_ref=None):
    mean, inverse, gain, shift = norm_rows(table_ref, which)
    mean_grad, mean_cross = back_means(sums, gain, pixels)
    slope = inverse * gain * (0.5 if double else 1.0)
    level, tilt = inverse * mean_grad, inverse * inverse * mean_cross
    if scales_ref is not None:
        for row, scales in enumerate((mean, slope, level, tilt)):
            scales_ref[row : row + 1, :] = scales

    def back(rows, inner):
        return total_ref[inner, :] * slope - level - (read(rows) - mean) * tilt

    return back


def own_lanes():
    block = lax.axis_index("height") // 2
    return pl.ds(pl.multiple_of(block * NARROW, NARROW), NARROW)


def narrow_back(total_ref, value_ref, scales_ref):
    lanes = own_lanes()
    mean, slope, level, tilt = (scales_ref[row : row + 1, lanes] for row in range(4))
    return total_ref[:, lanes] * slope - level - (value_ref[:, lanes] - mean) * tilt


def turn_kernel(grad_ref, mask_ref, weights_ref, total_ref, taps_ref, *, cols):
    begin_back(grad_ref, weights_ref.at[1], mask_ref, taps_ref, total_ref, cols)


def norm_rows(table_ref, which):
    picks = (2 * which, 2 * which + 1, 6 + which, 9 + which)
    return tuple(table_ref[pick : pick + 1, :] for pick in picks)


def build_masks(ids_ref, mask_ref, lanes_ref, id_rows_ref, id_cols_ref, cols):
    rows = ids_ref.shape[1]

    def one_row(row, carry):
        here = ids_ref[0, row]
        place = pl.ds(pl.multiple_of(row * cols, cols), cols)
        id_rows_ref[place, :] = jnp.full((cols, LANES), here, jnp.int32)
        for side, other in ((0, row - 1), (1, row + 1)):
            inside = jnp.logical_and(other >= 0, other < rows)
            other_id = ids_ref[0, jnp.clip(other, 0, rows - 1)]
            same = jnp.where(jnp.logical_and(inside, other_id == here), 1.0, 0.0)
            mask_ref[side, place, :] = jnp.full((cols, LANES), same, jnp.float32)
        return carry

    lax.fori_loop(0, rows, one_row, 0)
    lane = lax.broadcasted_iota(jnp.int32, (8, LANES), 1)
    each = LANES // cols
    for block in range(rows // each):
        ids = jnp.full((8, LANES), ids_ref[0, block * each], jnp.int32)
        for step in range(1, each):
            ids = jnp.where(lane >= step * cols, ids_ref[0, block * each + step], ids)
        id_cols_ref[:, block * LANES : (block + 1) * LANES] = ids
    ids = id_cols_ref[...].astype(jnp.float32)
    pixels = ids.shape[1]
    pixel = lax.broadcasted_iota(jnp.int32, ids.shape, 1)
    above = jnp.where(pixel < cols, -1.0, pltpu.roll(ids, cols, 1))
    below = jnp.where(pixel >= pixels - cols, -1.0, pltpu.roll(ids, pixels - cols, 1))
    lanes_ref[0:1, :] = jnp.where(above == ids, 1.0, 0.0)[0:1]
    lanes_ref[1:2, :] = jnp.where(below == ids, 1.0, 0.0)[0:1]


def place_pieces(pieces, whole_ref, sems):
    own_pixels = whole_ref.shape[0] // len(pieces)
    height = lax.axis_index("height")
    copies = []
    for place, piece in enumerate(pieces):
        piece = piece.at[piece.shape[0] - own_pixels : piece.shape[0], :]
        start = pl.multiple_of((height ^ place) * own_pixels, own_pixels)
        rows = pl.ds(start, own_pixels)
        copies.append(pltpu.make_async_copy(piece, whole_ref.at[rows, :], sems.at[place]))
    return copies


def hold_kernel(
    ids_hbm,
    gains_hbm,
    shifts_hbm,
    biases_hbm,
    weights_hbm,
    qkv_hbm,
    proj_hbm,
    qv_bias_hbm,
    proj_bias_hbm,
    weights_ref,
    turned_ref,
    qkv_ref,
    proj_ref,
    table_ref,
    mask_ref,
    lanes_ref,
    id_rows_ref,
    id_cols_ref,
    ids_ref,
    gains_ref,
    shifts_ref,
    biases_ref,
    qv_bias_ref,
    proj_bias_ref,
    sems,
    *,
    cols,
):
    channels = weights_ref.shape[-1]
    small = [
        (ids_hbm, ids_ref),
        (gains_hbm, gains_ref),
        (shifts_hbm, shifts_ref),
        (biases_hbm, biases_ref),
        (qv_bias_hbm, qv_bias_ref),
        (proj_bias_hbm, proj_bias_ref),
    ]
    large = [(weights_hbm, weights_ref), (qkv_hbm, qkv_ref), (proj_hbm, proj_ref)]
    for which in range(2):
        for row_tap in range(3):
            for col_tap in range(3):
                place = slice(col_tap * channels, (col_tap + 1) * channels)
                large.append(
                    (
                        weights_hbm.at[which, 2 - row_tap, 2 - col_tap],
                        turned_ref.at[which, row_tap, :, place],
                    )
                )
    copies = [
        pltpu.make_async_copy(source, target, sems.at[index])
        for index, (source, target) in enumerate(small + large)
    ]
    for copy in copies:
        copy.start()
    for copy in copies[: len(small)]:
        copy.wait()
    build_masks(ids_ref, mask_ref, lanes_ref, id_rows_ref, id_cols_ref, cols)
    table_ref[6:9, :] = gains_ref[...]
    table_ref[9:12, :] = shifts_ref[...]
    table_ref[12:14, :] = biases_ref[...]
    table_ref[14:16, :] = qv_bias_ref[...]
    table_ref[16:17, :] = proj_bias_ref[...]
    for copy in copies[len(small) :]:
        copy.wait()


def conv_kernel(*refs, cols, count):
    pieces, refs = refs[:count], refs[count:]
    (
        weights_ref,
        params_ref,
        mask_ref,
        features_ref,
        act_one_ref,
        middle_ref,
        act_two_ref,
        residual_ref,
        table_ref,
        own_ref,
        taps_ref,
        sem,
    ) = refs
    pixels, channels = features_ref.shape
    wide = jnp.float32
    own_copy = pltpu.make_async_copy(pieces[0], own_ref, sem)
    own_copy.start()
    table_ref[...] = params_ref[...]
    clear_edges(taps_ref, cols)

    def read_input(rows):
        return features_ref[rows, :].astype(wide)

    def read_middle(rows):
        return middle_ref[rows, :]

    height = lax.axis_index("height")
    own_pixels = pixels // count
    seen = RunningStats(channels)
    for place in list(range(1, count)) + [0]:
        if place == 0:
            own_copy.wait()
        piece = (pieces[place] if place else own_ref)[0:own_pixels, :]
        start = pl.multiple_of((height ^ place) * own_pixels, own_pixels)
        features_ref[pl.ds(start, own_pixels), :] = piece
        seen.add(piece.astype(wide))
    table_ref[0:1, :], table_ref[1:2, :] = seen.finish(pixels)
    seen = RunningStats(channels)

    def keep(rows, value):
        seen.add(value)
        return value

    run_conv(
        taps_ref,
        product_forward(weights_ref.at[0]),
        mask_ref,
        middle_ref,
        activation(read_input, *norm_rows(table_ref, 0), act_one_ref, taps_ref, cols),
        lambda rows, part: part + table_ref[12:13, :],
        keep,
        cols,
    )
    table_ref[2:3, :], table_ref[3:4, :] = seen.finish(pixels)
    seen = RunningStats(channels)
    run_conv(
        taps_ref,
        product_forward(weights_ref.at[1]),
        mask_ref,
        residual_ref,
        activation(read_middle, *norm_rows(table_ref, 1), act_two_ref, taps_ref, cols),
        lambda rows, part: part + (read_input(rows) + table_ref[13:14, :]),
        keep,
        cols,
    )
    table_ref[4:5, :], table_ref[5:6, :] = seen.finish(pixels)


def score_kernel(
    qkv_ref,
    proj_ref,
    residual_ref,
    table_ref,
    id_rows_ref,
    id_cols_ref,
    normed_ref,
    query_ref,
    key_ref,
    value_ref,
    soft_ref,
    out_flip_ref,
    output_ref,
    value_flip_ref,
    *scores_refs,
    score_scale,
):
    pixels, channels = residual_ref.shape
    own_pixels = output_ref.shape[0]
    wide = jnp.float32
    exponent = score_scale * 1.4426950408889634
    mean, inverse, gain, shift = norm_rows(table_ref, 2)
    scale = inverse * gain

    def normalise(start):
        rows = slice(start, start + KEY_ROWS)
        normed = (residual_ref[rows, :] - mean) * scale + shift
        normed_ref[rows, :] = normed.astype(jnp.bfloat16)

    def project(start):
        rows = slice(start, start + KEY_ROWS)
        normed = normed_ref[rows, :]
        query_ref[rows, :] = (
            jnp.dot(normed, qkv_ref[:, 0:channels], preferred_element_type=wide)
            + table_ref[14:15, :]
        ).astype(jnp.bfloat16)
        key_ref[rows, :] = jnp.dot(
            normed, qkv_ref[:, channels : 2 * channels], preferred_element_type=wide
        ).astype(jnp.bfloat16)
        values = (
            jnp.dot(normed, qkv_ref[:, 2 * channels :], preferred_element_type=wide)
            + table_ref[15:16, :]
        ).astype(jnp.bfloat16)
        value_ref[rows, :] = values
        value_flip_ref[:, rows] = values.T

    normalise(0)
    for start in range(0, pixels, KEY_ROWS):
        if start + KEY_ROWS < pixels:
            normalise(start + KEY_ROWS)
        project(start)
    block = scores_refs[0].shape[1]
    steps = range(0, pixels, KEY_ROWS)

    def score(index):
        rows = slice(index * block, (index + 1) * block)
        for start in steps:
            keys = slice(start, start + KEY_ROWS)
            scores = lax.dot_general(
                key_ref[keys, :],
                query_ref[rows, :],
                (((1,), (1,)), ((), ())),
                preferred_element_type=wide,
            )
            same = widen(id_rows_ref[keys, :], block) == id_cols_ref[0:1, rows]
            scores_refs[index][keys, :] = jnp.where(same, scores, masked_score)

    def soften(index):
        rows = slice(index * block, (index + 1) * block)
        scores_ref = scores_refs[index]
        peak = jnp.full((8, block), masked_score, wide)
        for start in steps:
            scores = scores_ref[start : start + KEY_ROWS, :]
            peak = jnp.maximum(peak, jnp.max(scores.reshape(-1, 8, block), axis=0))
        peak = jnp.max(peak, axis=0, keepdims=True)
        total = jnp.zeros((8, block), wide)
        for start in steps:
            keys = slice(start, start + KEY_ROWS)
            powers = jnp.exp2((scores_ref[keys, :] - peak) * exponent)
            scores_ref[keys, :] = powers
            total = total + fold(powers)
        share = 1.0 / column_total(total)
        for start in steps:
            keys = slice(start, start + KEY_ROWS)
            soft_ref[keys, rows] = (scores_ref[keys, :] * share).astype(jnp.bfloat16)

    score(0)
    for index in range(len(scores_refs)):
        if index + 1 < len(scores_refs):
            score(index + 1)
        soften(index)

    def collect(rows, carry):
        out_flip_ref[rows, :] = jnp.dot(
            value_flip_ref[rows, :], soft_ref[...], preferred_element_type=wide
        ).astype(jnp.bfloat16)
        return carry

    each_block(channels, channels // 2, collect)
    height = lax.axis_index("height")
    own = pl.ds(pl.multiple_of(height * own_pixels, own_pixels), own_pixels)
    output_ref[...] = (
        residual_ref[own, :]
        + lax.dot_general(
            out_flip_ref[:, own],
            proj_ref[...],
            (((0,), (0,)), ((), ())),
            preferred_element_type=wide,
        )
        + table_ref[16:17, :]
    ).astype(jnp.bfloat16)


def own_quarter():
    height = lax.axis_index("height")
    return (height & 1) * 2 + ((height >> 1) & 1)


def attention_kernel(
    proj_ref,
    normed_ref,
    query_ref,
    key_ref,
    value_ref,
    soft_ref,
    out_flip_ref,
    *refs,
    score_scale,
    count,
):
    pieces, (grad_ref, packed_ref, sums_ref), refs = (
        refs[:count],
        refs[count : count + 3],
        refs[count + 3 :],
    )
    pixels, channels = normed_ref.shape
    blocks = pixels // SCORE_ROWS
    grads_refs, refs = refs[-blocks:], refs[:-blocks]
    keep_ref, send_ref, mixed_ref, key_flip_ref, back_ref, score_grad_ref, flip_ref, sems = refs
    wide = jnp.float32
    copies = place_pieces(pieces, grad_ref, sems)
    for copy in copies:
        copy.start()
    quarter = channels // 4
    own = pl.ds(pl.multiple_of(own_quarter() * quarter, quarter), quarter)
    flip_ref[...] = normed_ref[:, own].T
    key_flip_ref[...] = key_ref[...].T
    for copy in copies:
        copy.wait()
    block, count = SCORE_ROWS, blocks
    steps = range(0, pixels, KEY_ROWS)

    def block_rows(index):
        return slice(index * block, (index + 1) * block)

    for index in range(count):
        back_ref[block_rows(index), :] = lax.dot_general(
            grad_ref[block_rows(index), :],
            proj_ref[...],
            (((1,), (1,)), ((), ())),
            preferred_element_type=wide,
        ).astype(jnp.bfloat16)

    def weigh(index):
        total = jnp.zeros((8, block), wide)
        for start in steps:
            keys = slice(start, start + KEY_ROWS)
            weight_grad = lax.dot_general(
                value_ref[keys, :],
                back_ref[block_rows(index), :],
                (((1,), (1,)), ((), ())),
                preferred_element_type=wide,
            )
            grads_refs[index][keys, :] = weight_grad
            total = total + fold(soft_ref[keys, block_rows(index)].astype(wide) * weight_grad)
        return column_total(total)

    def slope(index, dots):
        for start in steps:
            keys = slice(start, start + KEY_ROWS)
            weights = soft_ref[keys, block_rows(index)].astype(wide)
            score_grad_ref[keys, block_rows(index)] = (
                weights * (grads_refs[index][keys, :] - dots)
            ).astype(jnp.bfloat16)

    dots = weigh(0)
    for index in range(count):
        now, rows = dots, block_rows(index)
        if index + 1 < count:
            dots = weigh(index + 1)
        slope(index, now)
        packed_ref[rows, 2 * channels :] = jnp.dot(
            soft_ref[rows, :], back_ref[...], preferred_element_type=wide
        ).astype(jnp.bfloat16)
        query_grad = jnp.dot(
            key_flip_ref[...], score_grad_ref[:, rows], preferred_element_type=wide
        )
        packed_ref[rows, 0:channels] = (query_grad * score_scale).astype(jnp.bfloat16).T
    for index in range(count):
        rows = block_rows(index)
        packed_ref[rows, channels : 2 * channels] = (
            jnp.dot(score_grad_ref[rows, :], query_ref[...], preferred_element_type=wide)
            * score_scale
        ).astype(jnp.bfloat16)

    def pack(rows, carry):
        return (
            carry[0] + fold(packed_ref[rows, 0:channels].astype(wide)),
            carry[1] + fold(packed_ref[rows, 2 * channels :].astype(wide)),
            carry[2] + fold(grad_ref[rows, :].astype(wide)),
        )

    zeros = jnp.zeros((8, channels), wide)
    totals = zeros, zeros, zeros
    for start in range(0, pixels, CHUNK):
        totals = pack(pl.ds(start, CHUNK), totals)
    sums_ref[...] = jnp.zeros(sums_ref.shape, wide)
    for row, total in enumerate(totals):
        sums_ref[8 + row : 9 + row, :] = column_total(total)
    mixed_ref[:, 0 : 3 * channels] = jnp.dot(
        flip_ref[...], packed_ref[...], preferred_element_type=wide
    ).astype(jnp.bfloat16)
    mixed_ref[:, 3 * channels :] = jnp.dot(
        out_flip_ref[own, :], grad_ref[...], preferred_element_type=wide
    ).astype(jnp.bfloat16)
    keep_half(mixed_ref, 0, keep_ref, send_ref)


def third_kernel(
    qkv_ref,
    grad_ref,
    packed_ref,
    residual_ref,
    table_ref,
    act_two_ref,
    lanes_ref,
    old_sums_ref,
    residual_grad_ref,
    grad_two_ref,
    sums_ref,
    part_ref,
    total_ref,
    flip_ref,
    columns_ref,
    *,
    cols,
):
    pixels, channels = residual_ref.shape
    block = FILL_ROWS
    wide = jnp.float32
    mean, inverse, gain, shift = norm_rows(table_ref, 2)
    zeros = jnp.zeros((8, channels), wide)

    sums = (zeros, zeros)
    for start in range(0, pixels, block):
        rows = pl.ds(start, block)
        normed_grad = lax.dot_general(
            packed_ref[rows, :], qkv_ref[...], (((1,), (1,)), ((), ())), preferred_element_type=wide
        )
        total_ref[rows, :] = normed_grad
        centered = residual_ref[rows, :] - mean
        sums = sums[0] + fold(normed_grad), sums[1] + fold(normed_grad * centered)
    sums = sums[0], sums[1] * inverse
    sums_ref[...] = old_sums_ref[...]
    sums_ref[5:6, :] = column_total(sums[1])
    sums_ref[6:7, :] = column_total(sums[0])
    back = norm_back(
        total_ref, False, sums, lambda rows: residual_ref[rows, :], table_ref, 2, pixels
    )

    def finish(rows, carry):
        total = grad_ref[rows, :].astype(wide) + back(rows, rows)
        residual_grad_ref[rows, :] = total
        low = total.astype(jnp.bfloat16)
        grad_two_ref[rows, :] = low
        return carry + fold(low.astype(wide))

    sums_ref[7:8, :] = column_total(each_chunk(pixels, finish, zeros))
    narrow = grad_two_ref[:, own_lanes()]
    weight_part(act_two_ref, narrow, lanes_ref, flip_ref, columns_ref, part_ref, cols)


def second_kernel(
    old_total_ref,
    taps_ref,
    middle_ref,
    table_ref,
    act_one_ref,
    mask_ref,
    lanes_ref,
    weights_ref,
    old_sums_ref,
    part_two_ref,
    grad_one_ref,
    sums_ref,
    keep_one_ref,
    send_one_ref,
    keep_two_ref,
    send_two_ref,
    total_ref,
    flip_ref,
    columns_ref,
    part_ref,
    scales_ref,
    *,
    cols,
):
    pixels, channels = middle_ref.shape

    def read(rows):
        return middle_ref[rows, :]

    sums = finish_back(
        weights_ref.at[1], mask_ref, taps_ref, total_ref, read, table_ref, 1, cols, old_total_ref
    )
    back = norm_back(total_ref, True, sums, read, table_ref, 1, pixels, scales_ref)
    narrow = narrow_back(total_ref, middle_ref, scales_ref).astype(jnp.bfloat16)
    weight_part(act_one_ref, narrow, lanes_ref, flip_ref, columns_ref, part_ref, cols)
    sums_ref[...] = old_sums_ref[...]
    sums_ref[2:3, :] = column_total(sums[1])
    sums_ref[3:4, :] = column_total(sums[0])

    def finish(rows, carry):
        low = back(rows, rows).astype(jnp.bfloat16)
        grad_one_ref[rows, :] = low
        return carry + fold(low.astype(jnp.float32))

    zeros = jnp.zeros((8, channels), jnp.float32)
    sums_ref[4:5, :] = column_total(each_chunk(pixels, finish, zeros))
    keep_half(part_ref, 1, keep_one_ref, send_one_ref)
    keep_half(part_two_ref, 1, keep_two_ref, send_two_ref)


def near_far():
    core = lax.axis_index("height") & 1
    return 1 + core, 2 - core


def keep_half(source_ref, axis, keep_ref, send_ref):
    me = lax.axis_index("canvas")
    near, far = near_far()
    rows, width = keep_ref.shape[0] // 2, keep_ref.shape[1]
    for target_ref, flip in ((keep_ref, 0), (send_ref, near)):
        for slot, other in enumerate((0, far)):
            owner = me ^ flip ^ other
            target = target_ref.at[slot * rows : (slot + 1) * rows, :]
            if axis == 0:
                target[...] = source_ref[pl.ds(pl.multiple_of(owner * rows, rows), rows), :]
            else:
                target[...] = source_ref[:, pl.ds(pl.multiple_of(owner * width, width), width)]


def first_kernel(
    grad_one_ref,
    features_ref,
    table_ref,
    mask_ref,
    old_sums_ref,
    weights_ref,
    own_ref,
    sums_ref,
    partial_ref,
    total_ref,
    taps_ref,
    *,
    cols,
):
    def read(rows):
        return features_ref[rows, :].astype(jnp.float32)

    weights = weights_ref.at[0]
    begin_back(grad_one_ref, weights, mask_ref, taps_ref, total_ref, cols)
    sums = finish_back(weights, mask_ref, taps_ref, total_ref, read, table_ref, 0, cols)
    partial_ref[0:8, :], partial_ref[8:16, :] = sums
    sums_ref[...] = old_sums_ref[...]
    sums_ref[0:1, :] = column_total(sums[1])
    sums_ref[1:2, :] = column_total(sums[0])
    count = own_ref.shape[0]
    own = pl.ds(pl.multiple_of(lax.axis_index("height") * count, count), count)
    own_ref[...] = total_ref[own, :]


def own_kernel(
    own_ref, partial_ref, features_ref, residual_grad_ref, table_ref, input_grad_ref
):
    def read(rows):
        return features_ref[rows, :].astype(jnp.float32)

    sums = partial_ref[0:8, :], partial_ref[8:16, :]
    pixels = features_ref.shape[0]
    back = norm_back(own_ref, True, sums, read, table_ref, 0, pixels)
    count = own_ref.shape[0]
    own = pl.ds(pl.multiple_of(lax.axis_index("height") * count, count), count)
    total = residual_grad_ref[own, :] + back(own, slice(0, count))
    input_grad_ref[...] = total.astype(jnp.bfloat16)


def place_kernel(*refs):
    joints, packed_ref = refs[:-1], refs[-1]
    share = packed_ref.shape[0] // len(joints)
    me = lax.axis_index("canvas")
    for step, joint in enumerate(joints):
        place = pl.ds(pl.multiple_of((me ^ step) * share, share), share)
        packed_ref[place, :] = joint[...]


def cut_kernel(packed_ref, *half_refs):
    rows = half_refs[0].shape[0]
    for index, half_ref in enumerate(half_refs):
        half_ref[...] = packed_ref[index * rows : (index + 1) * rows, :]


def spread_quarters(packed, flips, qkv_ref, proj_ref, qkv_hbm, proj_hbm, sems):
    quarter = packed[0].shape[0]
    inner = qkv_ref.shape[2]
    copies = []
    for index, packed_ref in enumerate(packed):
        owner = own_quarter() ^ flips[index]
        rows = pl.ds(pl.multiple_of(owner * quarter, quarter), quarter)
        qkv_ref[index] = packed_ref[:, 0:inner].astype(jnp.float32)
        proj_ref[index] = packed_ref[:, inner:].astype(jnp.float32)
        for which, (held, target) in enumerate(((qkv_ref, qkv_hbm), (proj_ref, proj_hbm))):
            copy = pltpu.make_async_copy(held.at[index], target.at[rows, :], sems.at[index, which])
            copy.start()
            copies.append(copy)
    return copies


def join_kernel(*refs):
    packed, (qkv_hbm, proj_hbm, qkv_ref, proj_ref, sems) = refs[:-5], refs[-5:]
    copies = spread_quarters(packed, [0, 2], qkv_ref, proj_ref, qkv_hbm, proj_hbm, sems)
    for copy in copies:
        copy.wait()


def halve_kernel(keep_ref, got_ref, hold_ref, send_ref):
    total = keep_ref[...].astype(jnp.float32) + got_ref[...].astype(jnp.float32)
    rows = hold_ref.shape[0]
    hold_ref[...] = total[0:rows]
    send_ref[0:rows, :] = total[rows:].astype(jnp.bfloat16)


def halve_both_kernel(
    keep_ref, got_ref, keep_two_ref, got_two_ref, hold_ref, send_ref, hold_two_ref
):
    rows = hold_ref.shape[0]
    halve_kernel(keep_ref, got_ref, hold_ref, send_ref)
    halve_kernel(keep_two_ref, got_two_ref, hold_two_ref, send_ref.at[rows : 2 * rows, :])


def last_kernel(
    chip_ref,
    both_a_ref,
    both_b_ref,
    old_qkv,
    old_proj,
    qkv_hbm,
    proj_hbm,
    qkv_ref,
    proj_ref,
    sems,
):
    copies = []
    rows = both_a_ref.shape[0]
    inner = qkv_ref.shape[2]
    chips = (chip_ref.at[0:rows, :], chip_ref.at[rows : 2 * rows, :])
    for index, piece_ref in enumerate((*chips, both_a_ref, both_b_ref)):
        start = ((own_quarter() ^ (1 if index < 2 else 3)) * 2 + index % 2) * rows
        target = pl.ds(pl.multiple_of(start, rows), rows)
        qkv_ref[index] = piece_ref[:, 0:inner].astype(jnp.float32)
        proj_ref[index] = piece_ref[:, inner:].astype(jnp.float32)
        for which, (held, whole) in enumerate(((qkv_ref, qkv_hbm), (proj_ref, proj_hbm))):
            copy = pltpu.make_async_copy(held.at[index], whole.at[target, :], sems.at[index, which])
            copy.start()
            copies.append(copy)
    for copy in copies:
        copy.wait()


def sums_kernel(
    sums_ref,
    got_sums_ref,
    hold_one_ref,
    hold_two_ref,
    got_ref,
    share_ref,
    gains_ref,
    shifts_ref,
    conv_ref,
    qv_ref,
    bias_ref,
):
    rows = hold_one_ref.shape[0]
    for which, hold_ref in enumerate((hold_one_ref, hold_two_ref)):
        got = got_ref[which * rows : (which + 1) * rows, :].astype(jnp.float32)
        share_ref[which] = (hold_ref[...] + got).reshape(share_ref.shape[1:])
    total = sums_ref[...] + got_sums_ref[...]
    for row, start in enumerate((0, 2, 5)):
        gains_ref[row : row + 1, :] = total[start : start + 1]
        shifts_ref[row : row + 1, :] = total[start + 1 : start + 2]
    conv_ref[0:1, :] = total[4:5]
    conv_ref[1:2, :] = total[7:8]
    qv_ref[...] = total[8:10]
    bias_ref[...] = total[10:11]


def call_kernel(kernel, outputs, scratch, operands, places, flops, limit, out_places=None, aliases={}):
    out_places = out_places or "v" * len(outputs)
    spaces = {
        "v": pl.BlockSpec(memory_space=pltpu.VMEM),
        "s": pl.BlockSpec(memory_space=pltpu.SMEM),
        "h": pl.BlockSpec(memory_space=pl.ANY),
        "o": pl.BlockSpec(memory_space=pltpu.VMEM),
        "a": pl.BlockSpec(memory_space=pl.ANY),
    }
    moved = 8 * flops // LANES
    held = {"v": pltpu.VMEM, "h": pltpu.HBM, "o": jax.ShapeDtypeStruct}
    operands = [
        pltpu.with_memory_space_constraint(array, pltpu.HBM) if place == "h" else array
        for array, place in zip(operands, places)
    ]
    return pl.pallas_call(
        kernel,
        out_shape=[held[place](*output) for output, place in zip(outputs, out_places)],
        in_specs=[spaces[place] for place in places],
        out_specs=[spaces[place] for place in out_places],
        scratch_shapes=scratch,
        input_output_aliases=aliases,
        compiler_params=pltpu.CompilerParams(vmem_limit_bytes=limit * 2**20),
        cost_estimate=pl.CostEstimate(flops=flops, bytes_accessed=moved, transcendentals=0),
    )(*operands)


def send_height(block, step):
    size = lax.axis_size("height")
    return lax.ppermute(block, "height", [(i, i ^ step) for i in range(size)])


def with_cores(blocks, other):
    pieces = [blocks[0], other]
    for block in blocks[1:]:
        pieces += [block, send_height(block, 1)]
    return pieces


def send_canvas(block, step):
    size = lax.axis_size("canvas")
    return lax.ppermute(block, "canvas", [(i, i ^ step) for i in range(size)])


def send_phase(block, phase):
    canvases, size = lax.axis_size("canvas"), lax.axis_size("height")
    pairs = []
    for canvas in range(canvases):
        for height in range(size):
            step = 2 if (height ^ phase) & 1 else 1
            pairs.append((canvas * size + height, (canvas ^ step) * size + height))
    return lax.ppermute(block, ("canvas", "height"), pairs)


def trade_canvas(pieces):
    return [pieces[0]] + [send_canvas(piece, step) for step, piece in enumerate(pieces) if step]


def whole_canvas(
    features,
    tile_ids,
    norm_gains,
    norm_shifts,
    conv_weights,
    conv_biases,
    qkv_weight,
    qv_bias,
    proj_weight,
    proj_bias,
    cotangent,
):
    height_size = lax.axis_size("height")
    canvas_size = lax.axis_size("canvas")
    local_rows, cols, channels = features.shape[1:]
    all_rows = tile_ids.shape[1]
    pixels = all_rows * cols
    own_pixels = local_rows * cols
    out_share = channels // height_size
    ci_share = channels // canvas_size
    quarter = channels // 4
    row_share = quarter // canvas_size
    low, wide = jnp.bfloat16, jnp.float32

    own_features = features.reshape(own_pixels, channels)
    own_grad = cotangent.reshape(own_pixels, channels)
    steps = range(2, height_size, 2)
    held_features = [own_features] + [send_height(own_features, step) for step in steps]
    plane = ((pixels, channels), low)
    plane_wide = ((pixels, channels), wide)
    sums_shape = ((16, channels), wide)
    mixed_halves = [((2 * row_share, 4 * channels), low)] * 2
    taps = pltpu.VMEM((pixels + 2 * cols, 3 * channels), low)
    held_wide = pltpu.VMEM((pixels, channels), wide)
    flipped = pltpu.VMEM((channels, pixels), low)
    narrow = pltpu.VMEM((NARROW, pixels), low)
    columns = pltpu.VMEM((9 * out_share, pixels), low)
    part_held = pltpu.VMEM((9 * out_share, channels), low)
    sem = pltpu.SemaphoreType.DMA
    conv_flops = 2 * 9 * pixels * channels * channels
    dot_flops = 2 * pixels * channels * channels
    score_flops = 2 * pixels * pixels * channels
    scale = channels ** (-0.5)

    (
        held_conv,
        turned,
        held_qkv,
        held_proj,
        params,
        mask,
        lane_mask,
        id_rows,
        id_cols,
    ) = call_kernel(
        functools.partial(hold_kernel, cols=cols),
        [
            (conv_weights.shape, low),
            ((2, 3, channels, 3 * channels), low),
            (qkv_weight.shape, low),
            (proj_weight.shape, low),
            ((24, channels), wide),
            ((2, pixels, LANES), wide),
            ((8, pixels), wide),
            ((pixels, LANES), jnp.int32),
            ((8, pixels), jnp.int32),
        ],
        [
            pltpu.SMEM(tile_ids.shape, jnp.int32),
            pltpu.VMEM(norm_gains.shape, wide),
            pltpu.VMEM(norm_shifts.shape, wide),
            pltpu.VMEM(conv_biases.shape, wide),
            pltpu.VMEM(qv_bias.shape, wide),
            pltpu.VMEM((1, channels), wide),
            sem((27,)),
        ],
        [
            tile_ids,
            norm_gains,
            norm_shifts,
            conv_biases,
            conv_weights,
            qkv_weight,
            proj_weight,
            qv_bias,
            proj_bias.reshape(1, channels),
        ],
        "h" * 9,
        conv_flops,
        8,
    )
    held_features[1:] = [
        lax.optimization_barrier((params, block))[1] for block in held_features[1:]
    ]
    other_core = send_height(jnp.concatenate([own_features, own_grad], axis=0), 1)
    pieces = with_cores(held_features, other_core)
    far_grad, *pieces[4::2] = lax.optimization_barrier((own_grad, *held_features[2:]))
    held_grads = [own_grad, send_height(own_grad, 2)]
    held_grads[1], pieces[2] = lax.optimization_barrier((held_grads[1], held_features[1]))
    held_grads += [send_height(far_grad, step) for step in steps[1:]]

    all_features, act_one, middle, act_two, residual, table = call_kernel(
        functools.partial(conv_kernel, cols=cols, count=height_size),
        [plane, plane, plane_wide, plane, plane_wide, ((24, channels), wide)],
        [pltpu.VMEM((own_pixels, channels), low), taps, sem],
        [*pieces, held_conv, params, mask],
        "h" + "v" * (height_size + 2),
        2 * conv_flops,
        16,
    )
    residual, *held_grads = lax.optimization_barrier((residual, *held_grads))
    grad_pieces = with_cores(held_grads, other_core)
    normed, query, key, value, soft, out_flip, output = call_kernel(
        functools.partial(score_kernel, score_scale=scale),
        [
            plane,
            plane,
            plane,
            plane,
            ((pixels, pixels), low),
            ((channels, pixels), low),
            ((own_pixels, channels), low),
        ],
        [
            flipped,
            *[pltpu.VMEM((pixels, SCORE_ROWS), wide)] * (pixels // SCORE_ROWS),
        ],
        [
            held_qkv,
            held_proj,
            residual,
            table,
            id_rows,
            id_cols,
        ],
        "vvvvvv",
        3 * dot_flops + 2 * score_flops,
        20,
        "v" * 6 + "o",
    )
    normed, *grad_pieces = lax.optimization_barrier((normed, *grad_pieces))
    all_grad, packed, sums, keep_mixed, send_mixed = call_kernel(
        functools.partial(attention_kernel, score_scale=scale, count=height_size),
        [plane, ((pixels, 3 * channels), low), sums_shape, *mixed_halves],
        [
            pltpu.VMEM((quarter, 4 * channels), low),
            flipped,
            pltpu.VMEM((pixels, channels), low),
            pltpu.VMEM((pixels, pixels), low),
            pltpu.VMEM((quarter, pixels), low),
            sem((height_size,)),
            *[pltpu.VMEM((pixels, SCORE_ROWS), wide)] * (pixels // SCORE_ROWS),
        ],
        [held_proj, normed, query, key, value, soft, out_flip, *grad_pieces],
        "vvvvvvvh" + "a" * (height_size - 1),
        3 * dot_flops + 4 * score_flops,
        20,
    )
    got_mixed = send_phase(send_mixed, 0)
    residual_grad, grad_two, sums, part_two = call_kernel(
        functools.partial(third_kernel, cols=cols),
        [plane_wide, plane, sums_shape, ((9 * out_share, channels), low)],
        [held_wide, narrow, columns],
        [held_qkv, all_grad, packed, residual, table, act_two, lane_mask, sums],
        "vvvvvvvv",
        3 * dot_flops + conv_flops // height_size,
        16,
    )
    grad_two, got_mixed = lax.optimization_barrier((grad_two, got_mixed))
    hold_mixed, send_mixed = call_kernel(
        halve_kernel,
        [((row_share, 4 * channels), kind) for kind in (wide, low)],
        [],
        [keep_mixed, got_mixed],
        "vv",
        1,
        12,
    )
    got_mixed = send_phase(send_mixed, 1)
    grad_two, hold_mixed = lax.optimization_barrier((grad_two, hold_mixed))
    half_total, half_taps = call_kernel(
        functools.partial(turn_kernel, cols=cols),
        [plane_wide, (taps.shape, low)],
        [],
        [grad_two, mask, turned],
        "vvv",
        2 * conv_flops // 3,
        16,
    )
    half_total, got_mixed = lax.optimization_barrier((half_total, got_mixed))
    mixed_sum = (hold_mixed + got_mixed.astype(wide)).astype(low)
    joints = trade_canvas([mixed_sum] * canvas_size)
    halves = [((2 * 9 * out_share, ci_share), low)] * 4
    grad_one, sums, keep_one, send_one, keep_two, send_two = call_kernel(
        functools.partial(second_kernel, cols=cols),
        [plane, sums_shape, *halves],
        [held_wide, narrow, columns, part_held, pltpu.VMEM((8, channels), wide)],
        [half_total, half_taps, middle, table, act_one, mask, lane_mask, turned, sums, part_two],
        "v" * 10,
        conv_flops // 2,
        20,
    )
    grad_one, *joints = lax.optimization_barrier((grad_one, *joints))
    (own_mixed,) = call_kernel(
        place_kernel,
        [((quarter, 4 * channels), low)],
        [],
        joints,
        "v" * canvas_size,
        1,
        12,
    )
    own_mixed, send_one, send_two = lax.optimization_barrier((own_mixed, send_one, send_two))
    chip_mixed = send_height(own_mixed, 2)
    core_mixed = send_height(own_mixed, 1)
    got_one, got_two = send_phase(send_one, 0), send_phase(send_two, 0)
    own_total, sums, partial_sums = call_kernel(
        functools.partial(first_kernel, cols=cols),
        [((own_pixels, channels), wide), sums_shape, sums_shape],
        [held_wide, taps],
        [grad_one, all_features, table, mask, sums, turned],
        "vvvvvv",
        1,
        20,
    )
    got_sums, own_sums = send_phase(sums, 0), sums
    sums, core_mixed, got_one, got_two = lax.optimization_barrier(
        (sums, core_mixed, got_one, got_two)
    )
    share_rows = 9 * out_share
    hold_one, send_share, hold_two = call_kernel(
        halve_both_kernel,
        [
            ((share_rows, ci_share), wide),
            ((2 * share_rows, ci_share), low),
            ((share_rows, ci_share), wide),
        ],
        [],
        [keep_one, got_one, keep_two, got_two],
        "vvvv",
        1,
        12,
    )
    got_share = send_phase(send_share, 1)

    def widened(count, rows):
        return [
            pltpu.VMEM((count, rows, 3 * channels), wide),
            pltpu.VMEM((count, rows, channels), wide),
            sem((count, 2)),
        ]

    grad_shapes = [(qkv_weight.shape, wide), (proj_weight.shape, wide)]
    core_mixed, hold_one = lax.optimization_barrier((core_mixed, hold_one))
    qkv_grad, proj_grad = call_kernel(
        join_kernel,
        grad_shapes,
        widened(2, quarter),
        [own_mixed, core_mixed],
        "vv",
        1,
        12,
        "hh",
    )
    qkv_grad, chip_mixed, got_sums = lax.optimization_barrier((qkv_grad, chip_mixed, got_sums))
    sums = own_sums + got_sums
    got_sums = send_phase(sums, 1)
    chip_halves = call_kernel(
        cut_kernel,
        [((quarter // 2, 4 * channels), low)] * 2,
        [],
        [chip_mixed],
        "v",
        1,
        12,
    )
    both_halves = [send_height(half, 1) for half in chip_halves]
    qkv_grad, proj_grad = call_kernel(
        last_kernel,
        grad_shapes,
        widened(4, quarter // 2),
        [chip_mixed, *both_halves, qkv_grad, proj_grad],
        "vvvhh",
        1,
        12,
        "hh",
        {3: 0, 4: 1},
    )
    qkv_grad, own_total = lax.optimization_barrier((qkv_grad, own_total))
    (input_grad,) = call_kernel(
        own_kernel,
        [((own_pixels, channels), low)],
        [],
        [own_total, partial_sums, all_features, residual_grad, table],
        "vvvvv",
        dot_flops // 4,
        12,
        "o",
    )
    input_grad, got_share, got_sums = lax.optimization_barrier((input_grad, got_share, got_sums))
    vector_shapes = [norm_gains.shape, norm_shifts.shape, conv_biases.shape, qv_bias.shape]
    conv_grad, gains_grad, shifts_grad, biases_grad, qv_grad, proj_bias_grad = call_kernel(
        sums_kernel,
        [((2, 3, 3, out_share, ci_share), wide)]
        + [(shape, wide) for shape in vector_shapes + [(1, channels)]],
        [],
        [sums, got_sums, hold_one, hold_two, got_share],
        "vvvvv",
        1,
        12,
        "o" * 6,
    )
    own_shape = (1, local_rows, cols, channels)
    return (
        output.reshape(own_shape),
        input_grad.reshape(own_shape),
        gains_grad,
        shifts_grad,
        jnp.swapaxes(conv_grad, 3, 4),
        biases_grad,
        qkv_grad,
        qv_grad,
        proj_grad,
        proj_bias_grad.reshape(channels),
    )


def on_device(*arrays):
    features, tile_ids = arrays[0], arrays[1]
    local_rows, cols, channels = features.shape[1:]
    pixels = tile_ids.shape[1] * cols
    height_size, canvas_size = lax.axis_size("height"), lax.axis_size("canvas")
    powers = all(size & (size - 1) == 0 for size in (height_size, canvas_size, cols))
    fits = (
        powers
        and height_size > 2
        and canvas_size == 4
        and channels == LANES * canvas_size
        and pixels <= MOST_PIXELS
        and pixels % FILL_ROWS == 0
        and FILL_ROWS % CHUNK == 0
        and pixels % SCORE_ROWS == 0
        and pixels % KEY_ROWS == 0
        and (local_rows * cols) % LANES == 0
        and CHUNK % cols == 0
        and cols % 16 == 0
        and channels % (LANES * canvas_size) == 0
        and 2 * channels == NARROW * height_size
    )
    return whole_canvas(*arrays) if fits else split_canvas(*arrays)


def solution(mesh):
    in_specs = (
        P("canvas", "height", None, None),
        P("canvas", None),
        P(),
        P(),
        P(),
        P(),
        P(),
        P(),
        P(),
        P(),
        P("canvas", "height", None, None),
    )
    out_specs = (
        P("canvas", "height", None, None),
        P("canvas", "height", None, None),
        P(),
        P(),
        P(None, None, None, "canvas", "height"),
        P(),
        P(),
        P(),
        P(),
        P(),
    )
    return jax.shard_map(
        on_device, mesh=mesh, in_specs=in_specs, out_specs=out_specs, check_vma=False
    )
```

profile of v0, /device:TPU:0, one launch (start us, length us, event | category | flops | bytes accessed | tf_op | source)
XLA Modules:
  0.0 89.2 jit_solution(5478844604624024982)
XLA Ops:
  0.6 5.1 %collective-permute-start.5 = (bf16[128,512]{1,0:T(8,128)(2,1)}, bf16[128,512]{1,0:T(8,128)(2,1)S(1)}, u32[]{:S(2)}, u32[]{:S(2)}) collective-permute-start(bf16[128,512]{1,0:T(8,128)(2,1)} %bitcast.8), channel_id=1, source_target_pairs={{0,6},{1,7},{2,4},{3,5},{4,2},{5,3},{6,0},{7,1},{8,14},{9,15},{10,... | collective-permute-start | bytes 393224 | tf_op jit(solution)/shard_map/ppermute | solution.py:1326
  5.8 0.6 collective-permute-start.2
  6.4 1.4 %collective-permute-start.1 = (bf16[128,512]{1,0:T(8,128)(2,1)}, bf16[128,512]{1,0:T(8,128)(2,1)S(1)}, u32[]{:S(2)}, u32[]{:S(2)}) collective-permute-start(bf16[128,512]{1,0:T(8,128)(2,1)} %bitcast.13), channel_id=1, source_target_pairs={{0,2},{1,3},{2,0},{3,1},{4,6},{5,7},{6,4},{7,5},{8,10},{9,11},{10,... | collective-permute-start | bytes 393224 | tf_op jit(solution)/shard_map/ppermute | solution.py:1326
  7.8 1.0 %pad_maximum_fusion = bf16[256,512]{1,0:T(8,128)(2,1)S(1)} fusion(bf16[128,512]{1,0:T(8,128)(2,1)} %bitcast.14, bf16[128,512]{1,0:T(8,128)(2,1)} %bitcast.11), kind=kLoop, calls=%fused_computation | loop fusion | flops 524288 | bytes 524288 | tf_op jit(solution)/shard_map/concatenate | solution.py:1450
  8.9 7.4 %shard_map.186 = (bf16[2,3,3,512,512]{4,3,2,1,0:T(8,128)(2,1)S(1)}, bf16[2,3,512,1536]{3,2,1,0:T(8,128)(2,1)S(1)}, bf16[512,1536]{1,0:T(8,128)(2,1)S(1)}, bf16[5...) custom-call(s32[1,64]{1,0:T(1,128)} %ids_hbm.1, ...), custom_call_target="tpu_custom_call" | custom-call | flops 4831838208 | bytes 301989888 | tf_op jit(solution)/shard_map/pallas_call | solution.py:1312
  16.3 0.9 collective-permute-done.4.refs_4_
  17.2 0.5 collective-permute-start.6
  18.0 3.4 %collective-permute-start.9 = (bf16[128,512]{1,0:T(8,128)(2,1)S(1)}, bf16[128,512]{1,0:T(8,128)(2,1)S(1)}, u32[]{:S(2)}, u32[]{:S(2)}) collective-permute-start(bf16[128,512]{1,0:T(8,128)(2,1)S(1)} %bitcast.16), channel_id=1, source_target_pairs={{0,6},{1,7},{2,4},{3,5},{4,2},{5,3},{6,0},{7,1},{8,14},{9,15},{10,... | collective-permute-start | bytes 393224 | tf_op jit(solution)/shard_map/ppermute | solution.py:1326
  21.4 13.1 %shard_map.187 = (bf16[1024,512]{1,0:T(8,128)(2,1)S(1)}, bf16[1024,512]{1,0:T(8,128)(2,1)S(1)}, f32[1024,512]{1,0:T(8,128)S(1)}, bf16[1024,512]{1,0:T(8,128)(2,1...) custom-call(bf16[128,512]{1,0:T(8,128)(2,1)} %bitcast.12, bf16[256,512]{1,0:T(8,128)(2,1)S(1)} %collective-permute-done.refs_1_, ...), custom_call_target="tpu_custom_call" | custom-call | flops 9663676416 | bytes 603979776 | tf_op jit(solution)/shard_map/pallas_call | solution.py:1312
  35.1 6.4 %shard_map.188 = (bf16[1024,512]{1,0:T(8,128)(2,1)S(1)}, bf16[1024,512]{1,0:T(8,128)(2,1)S(1)}, bf16[1024,512]{1,0:T(8,128)(2,1)S(1)}, bf16[1024,512]{1,0:T(8,12...) custom-call(bf16[512,1536]{1,0:T(8,128)(2,1)S(1)} %get-tuple-element.118.qkv_re, ...), custom_call_target="tpu_custom_call" | custom-call | flops 3758096384 | bytes 234881024 | tf_op jit(solution)/shard_map/pallas_call | solution.py:1312
  41.6 7.5 %shard_map.189 = (bf16[1024,512]{1,0:T(8,128)(2,1)S(1)}, bf16[1024,1536]{1,0:T(8,128)(2,1)S(1)}, f32[16,512]{1,0:T(8,128)S(1)}, bf16[64,2048]{1,0:T(8,128)(2,1)S(1)}, bf16[64,2048]{1,0:T(8,128)(2,1)S(1)}) custom-call(bf16[512,512]{1,0:T(8,128)(2,1)S(1)} %get-tuple-element.119.proj_ref, bf16[1024,512]{1,0:T(8,128)(2,1)S(1)} %get-tuple-element.142.normed_ref, ...), custom_call_target="tpu_custom_call" | custom-call | flops 5905580032 | bytes 369098752 | tf_op jit(solution)/shard_map/pallas_call | solution.py:1312
  49.1 1.6 %collective-permute-start.13 = (bf16[64,2048]{1,0:T(8,128)(2,1)S(1)}, bf16[64,2048]{1,0:T(8,128)(2,1)S(1)}, u32[]{:S(2)}, u32[]{:S(2)}) collective-permute-start(bf16[64,2048]{1,0:T(8,128)(2,1)S(1)} %get-tuple-element.162), channel_id=1, source_target_pairs={{0,8},{1,17},{2,10},{3,19},{4,12},{5,21},{6,14},{7,23},{8,0},{9,25... | collective-permute-start | bytes 786440 | tf_op jit(solution)/shard_map/ppermute | solution.py:1348
  50.6 4.3 %shard_map.190 = (f32[1024,512]{1,0:T(8,128)S(1)}, bf16[1024,512]{1,0:T(8,128)(2,1)S(1)}, f32[16,512]{1,0:T(8,128)S(1)}, bf16[576,512]{1,0:T(8,128)(2,1)S(1)}) custom-call(bf16[512,1536]{1,0:T(8,128)(2,1)S(1)} %get-tuple-element.118.qkv_ref, bf16[1024,512]{1,0:T(8,128)(2,1)S(1)} %get-tuple-element.156.grad_ref, ...), custom_call_target="tpu_custom_call" | custom-call | flops 2214592512 | bytes 138412032 | tf_op jit(solution)/shard_map/pallas_call | solution.py:1312
  55.0 0.6 collective-permute-done.13.got_ref
  55.6 1.6 %collective-permute-start.14 = (bf16[32,2048]{1,0:T(8,128)(2,1)S(1)}, bf16[32,2048]{1,0:T(8,128)(2,1)S(1)}, u32[]{:S(2)}, u32[]{:S(2)}) collective-permute-start(bf16[32,2048]{1,0:T(8,128)(2,1)S(1)} %get-tuple-element.170), channel_id=1, source_target_pairs={{0,16},{1,9},{2,18},{3,11},{4,20},{5,13},{6,22},{7,15},{8,24},{9,1... | collective-permute-start | bytes 393224 | tf_op jit(solution)/shard_map/ppermute | solution.py:1348
  57.2 3.5 %shard_map.192 = (f32[1024,512]{1,0:T(8,128)S(1)}, bf16[1056,1536]{1,0:T(8,128)(2,1)S(1)}) custom-call(bf16[1024,512]{1,0:T(8,128)(2,1)S(1)} %get-tuple-element.167.grad_ref, f32[2,1024,128]{2,1,0:T(8,128)S(1)} %get-tuple-element.128.refs_10_.mask_ref, bf16[2,3,512,1536]{3,2,1,0:T(8,128)(2,1)S(1)} %get-tuple-element.168.weights_ref), custom_call_target="tpu_custom_call" | custom-call | flops 3221225472 | bytes 201326592 | tf_op jit(solution)/shard_map/pallas_call | solution.py:1312
  60.7 2.5 %collective-permute-start.17 = (bf16[32,2048]{1,0:T(8,128)(2,1)S(1)}, bf16[32,2048]{1,0:T(8,128)(2,1)S(1)}, u32[]{:S(2)}, u32[]{:S(2)}) collective-permute-start(bf16[32,2048]{1,0:T(8,128)(2,1)S(1)} %add_convert_fusion.refs_0_), channel_id=1, source_target_pairs={{0,24},{8,16},{16,8},{24,0},{1,25},{9,17},{17,9},{25,1},{2,26},{10... | collective-permute-start | bytes 393224 | tf_op jit(solution)/shard_map/ppermute | solution.py:1338
  63.2 0.6 collective-permute-start.16
  63.7 0.5 collective-permute-start.15
  64.3 4.8 %shard_map.193 = (bf16[1024,512]{1,0:T(8,128)(2,1)S(1)}, f32[16,512]{1,0:T(8,128)S(1)}, bf16[1152,128]{1,0:T(8,128)(2,1)S(1)}, bf16[1152,128]{1,0:T(8,128)(2,1)S...) custom-call(f32[1024,512]{1,0:T(8,128)S(1)} %get-tuple-element.171.old_total_ref, ...), custom_call_target="tpu_custom_call" | custom-call | flops 2415919104 | bytes 150994944 | tf_op jit(solution)/shard_map/pallas_call | solution.py:1312
  69.4 1.1 %collective-permute-start.21 = (bf16[128,2048]{1,0:T(8,128)(2,1)S(1)}, bf16[128,2048]{1,0:T(8,128)(2,1)S(1)}, u32[]{:S(2)}, u32[]{:S(2)}) collective-permute-start(bf16[128,2048]{1,0:T(8,128)(2,1)S(1)} %shard_map.194.refs_0_), channel_id=1, source_target_pairs={{0,2},{1,3},{2,0},{3,1},{4,6},{5,7},{6,4},{7,5},{8,10},{9,11},{10,... | collective-permute-start | bytes 1572872 | tf_op jit(solution)/shard_map/ppermute | solution.py:1326
  70.5 1.4 %collective-permute-start.19 = (bf16[1152,128]{1,0:T(8,128)(2,1)S(1)}, bf16[1152,128]{1,0:T(8,128)(2,1)S(1)}, u32[]{:S(2)}, u32[]{:S(2)}) collective-permute-start(bf16[1152,128]{1,0:T(8,128)(2,1)S(1)} %get-tuple-element.191), channel_id=1, source_target_pairs={{0,8},{1,17},{2,10},{3,19},{4,12},{5,21},{6,14},{7,23},{8,0},{9,25... | collective-permute-start | bytes 884744 | tf_op jit(solution)/shard_map/ppermute | solution.py:1348
  71.9 0.6 collective-permute-start.20
  72.5 5.7 %shard_map.195 = (f32[128,512]{1,0:T(8,128)S(1)}, f32[16,512]{1,0:T(8,128)S(1)}, f32[16,512]{1,0:T(8,128)S(1)}) custom-call(bf16[1024,512]{1,0:T(8,128)(2,1)S(1)} %get-tuple-element.187.grad_one_ref, bf16[1024,512]{1,0:T(8,128)(2,1)S(1)} %get-tuple-element.188.features_ref, f32[24,512]{1,0:T(8,128)S(1)} %get-tuple-element.133.table_ref, ...), custom_call_target="tpu_custom_call" | custom-call | flops 1 | tf_op jit(solution)/shard_map/pallas_call | solution.py:1312
  78.2 1.4 %collective-permute-start.22 = (f32[16,512]{1,0:T(8,128)S(1)}, f32[16,512]{1,0:T(8,128)S(1)}, u32[]{:S(2)}, u32[]{:S(2)}) collective-permute-start(f32[16,512]{1,0:T(8,128)S(1)} %get-tuple-element.190), channel_id=1, source_target_pairs={{0,8},{1,17},{2,10},{3,19},{4,12},{5,21},{6,14},{7,23},{8,0},{9,25... | collective-permute-start | bytes 98312 | tf_op jit(solution)/shard_map/ppermute | solution.py:1348
  79.7 0.7 collective-permute-done.20.got_two_ref
  80.5 1.4 %collective-permute-start.25 = (bf16[1152,128]{1,0:T(8,128)(2,1)S(1)}, bf16[1152,128]{1,0:T(8,128)(2,1)S(1)}, u32[]{:S(2)}, u32[]{:S(2)}) collective-permute-start(bf16[1152,128]{1,0:T(8,128)(2,1)S(1)} %get-tuple-element.211), channel_id=1, source_target_pairs={{0,16},{1,9},{2,18},{3,11},{4,20},{5,13},{6,22},{7,15},{8,24},{9,1... | collective-permute-start | bytes 884744 | tf_op jit(solution)/shard_map/ppermute | solution.py:1348
  81.9 1.4 %shard_map.197 = (f32[512,1536]{1,0:T(8,128)}, f32[512,512]{1,0:T(8,128)}) custom-call(bf16[128,2048]{1,0:T(8,128)(2,1)S(1)} %shard_map.194.refs_0_, bf16[128,2048]{1,0:T(8,128)(2,1)S(1)} %collective-permute-done.18.refs_1_), custom_call_target="tpu_custom_call" | custom-call | flops 1 | tf_op jit(solution)/shard_map/pallas_call | solution.py:1312
  84.4 1.3 %collective-permute-start.26 = (f32[16,512]{1,0:T(8,128)S(1)}, f32[16,512]{1,0:T(8,128)S(1)}, u32[]{:S(2)}, u32[]{:S(2)}) collective-permute-start(f32[16,512]{1,0:T(8,128)S(1)} %add.7.sums_ref), channel_id=1, source_target_pairs={{0,16},{1,9},{2,18},{3,11},{4,20},{5,13},{6,22},{7,15},{8,24},{9,1... | collective-permute-start | bytes 98312 | tf_op jit(solution)/shard_map/ppermute | solution.py:1348
  85.8 1.4 %shard_map.199 = (f32[512,1536]{1,0:T(8,128)}, f32[512,512]{1,0:T(8,128)}) custom-call(bf16[128,2048]{1,0:T(8,128)(2,1)S(1)} %collective-permute-done.21.packed_ref.chip_ref, bf16[64,2048]{1,0:T(8,128)(2,1)S(1)} %collective-permute-done.23.both_a_ref, ...), custom_call_target="tpu_custom_call", output_to_operand_aliasing={{0}: (3, {}), {1}: (4, {})} | custom-call | flops 1 | tf_op jit(solution)/shard_map/pallas_call | solution.py:1312
  87.2 1.1 %shard_map.200 = bf16[128,512]{1,0:T(8,128)(2,1)} custom-call(f32[128,512]{1,0:T(8,128)S(1)} %get-tuple-element.208.own_ref, f32[16,512]{1,0:T(8,128)S(1)} %get-tuple-element.209.partial_ref, bf16[1024,512]{1,0:T(8,128)(2,1)S(1)} %get-tuple-element.188.features_ref, f32[1024,512]{1,0:T(8,128)S(1)} %get-tuple-element.210.residual_grad_ref, ...), custom_call_target="tpu_custom_call" | custom-call | flops 134217728 | bytes 8388608 | tf_op jit(solution)/shard_map/pallas_call | solution.py:1312
  88.3 0.9 shard_map.201
  (43 shorter events, 2.8 us)
Async XLA Ops:
  0.6 15.6 %collective-permute-start.5 = (bf16[128,512]{1,0:T(8,128)(2,1)}, bf16[128,512]{1,0:T(8,128)(2,1)S(1)}, u32[]{:S(2)}, u32[]{:S(2)}) collective-permute-start(bf16[128,512]{1,0:T(8,128)(2,1)} %bitcast.8), channel_id=1, source_target_pairs={{0,6},{1,7},{2,4},{3,5},{4,2},{5,3},{6,0},{7,1},{8,14},{9,15},{10,... | collective-permute-start | bytes 393224 | tf_op jit(solution)/shard_map/ppermute | solution.py:1326
  5.8 11.4 %collective-permute-start.4 = (bf16[128,512]{1,0:T(8,128)(2,1)}, bf16[128,512]{1,0:T(8,128)(2,1)S(1)}, u32[]{:S(2)}, u32[]{:S(2)}) collective-permute-start(bf16[128,512]{1,0:T(8,128)(2,1)} %bitcast.9), channel_id=1, source_target_pairs={{0,4},{1,5},{2,6},{3,7},{4,0},{5,1},{6,2},{7,3},{8,12},{9,13},{10,... | collective-permute-start | bytes 393224 | tf_op jit(solution)/shard_map/ppermute | solution.py:1326
  5.8 11.4 %collective-permute-start.2 = (bf16[128,512]{1,0:T(8,128)(2,1)}, bf16[128,512]{1,0:T(8,128)(2,1)S(1)}, u32[]{:S(2)}, u32[]{:S(2)}) collective-permute-start(bf16[128,512]{1,0:T(8,128)(2,1)} %bitcast.10), channel_id=1, source_target_pairs={{0,2},{1,3},{2,0},{3,1},{4,6},{5,7},{6,4},{7,5},{8,10},{9,11},{10,... | collective-permute-start | bytes 393224 | tf_op jit(solution)/shard_map/ppermute | solution.py:1326
  6.4 11.6 %collective-permute-start.1 = (bf16[128,512]{1,0:T(8,128)(2,1)}, bf16[128,512]{1,0:T(8,128)(2,1)S(1)}, u32[]{:S(2)}, u32[]{:S(2)}) collective-permute-start(bf16[128,512]{1,0:T(8,128)(2,1)} %bitcast.13), channel_id=1, source_target_pairs={{0,2},{1,3},{2,0},{3,1},{4,6},{5,7},{6,4},{7,5},{8,10},{9,11},{10,... | collective-permute-start | bytes 393224 | tf_op jit(solution)/shard_map/ppermute | solution.py:1326
  8.8 12.6 %collective-permute-start = (bf16[256,512]{1,0:T(8,128)(2,1)S(1)}, bf16[256,512]{1,0:T(8,128)(2,1)S(1)}, u32[]{:S(2)}, u32[]{:S(2)}) collective-permute-start(bf16[256,512]{1,0:T(8,128)(2,1)S(1)} %pad_maximum_fusion), channel_id=1, source_target_pairs={{0,1},{1,0},{2,3},{3,2},{4,5},{5,4},{6,7},{7,6},{8,9},{9,8},{10,11... | collective-permute-start | bytes 786440 | tf_op jit(solution)/shard_map/ppermute | solution.py:1326
  8.9 9.1 %copy-start = (bf16[1,8,16,512]{3,2,1,0:T(8,128)(2,1)S(1)}, bf16[1,8,16,512]{3,2,1,0:T(8,128)(2,1)}, u32[]{:S(2)}) copy-start(bf16[1,8,16,512]{3,2,1,0:T(8,128)(2,1)} %param.21) | copy-start | bytes 393220
  17.1 4.2 %collective-permute-start.3 = (bf16[128,512]{1,0:T(8,128)(2,1)S(1)}, bf16[128,512]{1,0:T(8,128)(2,1)S(1)}, u32[]{:S(2)}, u32[]{:S(2)}) collective-permute-start(bf16[128,512]{1,0:T(8,128)(2,1)S(1)} %collective-permute-done.2.refs_2_), channel_id=1, source_target_pairs={{0,1},{1,0},{2,3},{3,2},{4,5},{5,4},{6,7},{7,6},{8,9},{9,8},{10,11... | collective-permute-start | bytes 393224 | tf_op jit(solution)/shard_map/ppermute | solution.py:1326
  17.2 4.2 %collective-permute-start.6 = (bf16[128,512]{1,0:T(8,128)(2,1)S(1)}, bf16[128,512]{1,0:T(8,128)(2,1)S(1)}, u32[]{:S(2)}, u32[]{:S(2)}) collective-permute-start(bf16[128,512]{1,0:T(8,128)(2,1)S(1)} %collective-permute-done.4.refs_4_), channel_id=1, source_target_pairs={{0,1},{1,0},{2,3},{3,2},{4,5},{5,4},{6,7},{7,6},{8,9},{9,8},{10,11... | collective-permute-start | bytes 393224 | tf_op jit(solution)/shard_map/ppermute | solution.py:1326
  17.7 3.7 %collective-permute-start.7 = (bf16[128,512]{1,0:T(8,128)(2,1)S(1)}, bf16[128,512]{1,0:T(8,128)(2,1)S(1)}, u32[]{:S(2)}, u32[]{:S(2)}) collective-permute-start(bf16[128,512]{1,0:T(8,128)(2,1)S(1)} %collective-permute-done.5.refs_6_), channel_id=1, source_target_pairs={{0,1},{1,0},{2,3},{3,2},{4,5},{5,4},{6,7},{7,6},{8,9},{9,8},{10,11... | collective-permute-start | bytes 393224 | tf_op jit(solution)/shard_map/ppermute | solution.py:1326
  18.0 16.5 %collective-permute-start.9 = (bf16[128,512]{1,0:T(8,128)(2,1)S(1)}, bf16[128,512]{1,0:T(8,128)(2,1)S(1)}, u32[]{:S(2)}, u32[]{:S(2)}) collective-permute-start(bf16[128,512]{1,0:T(8,128)(2,1)S(1)} %bitcast.16), channel_id=1, source_target_pairs={{0,6},{1,7},{2,4},{3,5},{4,2},{5,3},{6,0},{7,1},{8,14},{9,15},{10,... | collective-permute-start | bytes 393224 | tf_op jit(solution)/shard_map/ppermute | solution.py:1326
  21.4 13.1 %collective-permute-start.8 = (bf16[128,512]{1,0:T(8,128)(2,1)S(1)}, bf16[128,512]{1,0:T(8,128)(2,1)S(1)}, u32[]{:S(2)}, u32[]{:S(2)}) collective-permute-start(bf16[128,512]{1,0:T(8,128)(2,1)S(1)} %bitcast.17), channel_id=1, source_target_pairs={{0,4},{1,5},{2,6},{3,7},{4,0},{5,1},{6,2},{7,3},{8,12},{9,13},{10,... | collective-permute-start | bytes 393224 | tf_op jit(solution)/shard_map/ppermute | solution.py:1326
  34.5 7.1 %collective-permute-start.10 = (bf16[128,512]{1,0:T(8,128)(2,1)S(1)}, bf16[128,512]{1,0:T(8,128)(2,1)S(1)}, u32[]{:S(2)}, u32[]{:S(2)}) collective-permute-start(bf16[128,512]{1,0:T(8,128)(2,1)S(1)} %collective-permute-done.1.refs_2_), channel_id=1, source_target_pairs={{0,1},{1,0},{2,3},{3,2},{4,5},{5,4},{6,7},{7,6},{8,9},{9,8},{10,11... | collective-permute-start | bytes 393224 | tf_op jit(solution)/shard_map/ppermute | solution.py:1326
  34.6 7.0 %collective-permute-start.11 = (bf16[128,512]{1,0:T(8,128)(2,1)S(1)}, bf16[128,512]{1,0:T(8,128)(2,1)S(1)}, u32[]{:S(2)}, u32[]{:S(2)}) collective-permute-start(bf16[128,512]{1,0:T(8,128)(2,1)S(1)} %collective-permute-done.8.refs_4_), channel_id=1, source_target_pairs={{0,1},{1,0},{2,3},{3,2},{4,5},{5,4},{6,7},{7,6},{8,9},{9,8},{10,11... | collective-permute-start | bytes 393224 | tf_op jit(solution)/shard_map/ppermute | solution.py:1326
  35.0 6.5 %collective-permute-start.12 = (bf16[128,512]{1,0:T(8,128)(2,1)S(1)}, bf16[128,512]{1,0:T(8,128)(2,1)S(1)}, u32[]{:S(2)}, u32[]{:S(2)}) collective-permute-start(bf16[128,512]{1,0:T(8,128)(2,1)S(1)} %collective-permute-done.9.refs_6_), channel_id=1, source_target_pairs={{0,1},{1,0},{2,3},{3,2},{4,5},{5,4},{6,7},{7,6},{8,9},{9,8},{10,11... | collective-permute-start | bytes 393224 | tf_op jit(solution)/shard_map/ppermute | solution.py:1326
  49.1 6.4 %collective-permute-start.13 = (bf16[64,2048]{1,0:T(8,128)(2,1)S(1)}, bf16[64,2048]{1,0:T(8,128)(2,1)S(1)}, u32[]{:S(2)}, u32[]{:S(2)}) collective-permute-start(bf16[64,2048]{1,0:T(8,128)(2,1)S(1)} %get-tuple-element.162), channel_id=1, source_target_pairs={{0,8},{1,17},{2,10},{3,19},{4,12},{5,21},{6,14},{7,23},{8,0},{9,25... | collective-permute-start | bytes 786440 | tf_op jit(solution)/shard_map/ppermute | solution.py:1348
  55.6 5.1 %collective-permute-start.14 = (bf16[32,2048]{1,0:T(8,128)(2,1)S(1)}, bf16[32,2048]{1,0:T(8,128)(2,1)S(1)}, u32[]{:S(2)}, u32[]{:S(2)}) collective-permute-start(bf16[32,2048]{1,0:T(8,128)(2,1)S(1)} %get-tuple-element.170), channel_id=1, source_target_pairs={{0,16},{1,9},{2,18},{3,11},{4,20},{5,13},{6,22},{7,15},{8,24},{9,1... | collective-permute-start | bytes 393224 | tf_op jit(solution)/shard_map/ppermute | solution.py:1348
  60.7 8.4 %collective-permute-start.17 = (bf16[32,2048]{1,0:T(8,128)(2,1)S(1)}, bf16[32,2048]{1,0:T(8,128)(2,1)S(1)}, u32[]{:S(2)}, u32[]{:S(2)}) collective-permute-start(bf16[32,2048]{1,0:T(8,128)(2,1)S(1)} %add_convert_fusion.refs_0_), channel_id=1, source_target_pairs={{0,24},{8,16},{16,8},{24,0},{1,25},{9,17},{17,9},{25,1},{2,26},{10... | collective-permute-start | bytes 393224 | tf_op jit(solution)/shard_map/ppermute | solution.py:1338
  63.2 6.1 %collective-permute-start.16 = (bf16[32,2048]{1,0:T(8,128)(2,1)S(1)}, bf16[32,2048]{1,0:T(8,128)(2,1)S(1)}, u32[]{:S(2)}, u32[]{:S(2)}) collective-permute-start(bf16[32,2048]{1,0:T(8,128)(2,1)S(1)} %add_convert_fusion.refs_0_), channel_id=1, source_target_pairs={{0,16},{8,24},{16,0},{24,8},{1,17},{9,25},{17,1},{25,9},{2,18},{10... | collective-permute-start | bytes 393224 | tf_op jit(solution)/shard_map/ppermute | solution.py:1338
  63.7 5.5 %collective-permute-start.15 = (bf16[32,2048]{1,0:T(8,128)(2,1)S(1)}, bf16[32,2048]{1,0:T(8,128)(2,1)S(1)}, u32[]{:S(2)}, u32[]{:S(2)}) collective-permute-start(bf16[32,2048]{1,0:T(8,128)(2,1)S(1)} %add_convert_fusion.refs_0_), channel_id=1, source_target_pairs={{0,8},{8,0},{16,24},{24,16},{1,9},{9,1},{17,25},{25,17},{2,10},{10... | collective-permute-start | bytes 393224 | tf_op jit(solution)/shard_map/ppermute | solution.py:1338
  69.3 11.0 %collective-permute-start.18 = (bf16[128,2048]{1,0:T(8,128)(2,1)S(1)}, bf16[128,2048]{1,0:T(8,128)(2,1)S(1)}, u32[]{:S(2)}, u32[]{:S(2)}) collective-permute-start(bf16[128,2048]{1,0:T(8,128)(2,1)S(1)} %shard_map.194.refs_0_), channel_id=1, source_target_pairs={{0,1},{1,0},{2,3},{3,2},{4,5},{5,4},{6,7},{7,6},{8,9},{9,8},{10,11... | collective-permute-start | bytes 1572872 | tf_op jit(solution)/shard_map/ppermute | solution.py:1326
  69.4 14.3 %collective-permute-start.21 = (bf16[128,2048]{1,0:T(8,128)(2,1)S(1)}, bf16[128,2048]{1,0:T(8,128)(2,1)S(1)}, u32[]{:S(2)}, u32[]{:S(2)}) collective-permute-start(bf16[128,2048]{1,0:T(8,128)(2,1)S(1)} %shard_map.194.refs_0_), channel_id=1, source_target_pairs={{0,2},{1,3},{2,0},{3,1},{4,6},{5,7},{6,4},{7,5},{8,10},{9,11},{10,... | collective-permute-start | bytes 1572872 | tf_op jit(solution)/shard_map/ppermute | solution.py:1326
  70.5 9.2 %collective-permute-start.19 = (bf16[1152,128]{1,0:T(8,128)(2,1)S(1)}, bf16[1152,128]{1,0:T(8,128)(2,1)S(1)}, u32[]{:S(2)}, u32[]{:S(2)}) collective-permute-start(bf16[1152,128]{1,0:T(8,128)(2,1)S(1)} %get-tuple-element.191), channel_id=1, source_target_pairs={{0,8},{1,17},{2,10},{3,19},{4,12},{5,21},{6,14},{7,23},{8,0},{9,25... | collective-permute-start | bytes 884744 | tf_op jit(solution)/shard_map/ppermute | solution.py:1348
  71.9 8.5 %collective-permute-start.20 = (bf16[1152,128]{1,0:T(8,128)(2,1)S(1)}, bf16[1152,128]{1,0:T(8,128)(2,1)S(1)}, u32[]{:S(2)}, u32[]{:S(2)}) collective-permute-start(bf16[1152,128]{1,0:T(8,128)(2,1)S(1)} %get-tuple-element.192), channel_id=1, source_target_pairs={{0,8},{1,17},{2,10},{3,19},{4,12},{5,21},{6,14},{7,23},{8,0},{9,25... | collective-permute-start | bytes 884744 | tf_op jit(solution)/shard_map/ppermute | solution.py:1348
  78.2 5.0 %collective-permute-start.22 = (f32[16,512]{1,0:T(8,128)S(1)}, f32[16,512]{1,0:T(8,128)S(1)}, u32[]{:S(2)}, u32[]{:S(2)}) collective-permute-start(f32[16,512]{1,0:T(8,128)S(1)} %get-tuple-element.190), channel_id=1, source_target_pairs={{0,8},{1,17},{2,10},{3,19},{4,12},{5,21},{6,14},{7,23},{8,0},{9,25... | collective-permute-start | bytes 98312 | tf_op jit(solution)/shard_map/ppermute | solution.py:1348
  80.5 7.8 %collective-permute-start.25 = (bf16[1152,128]{1,0:T(8,128)(2,1)S(1)}, bf16[1152,128]{1,0:T(8,128)(2,1)S(1)}, u32[]{:S(2)}, u32[]{:S(2)}) collective-permute-start(bf16[1152,128]{1,0:T(8,128)(2,1)S(1)} %get-tuple-element.211), channel_id=1, source_target_pairs={{0,16},{1,9},{2,18},{3,11},{4,20},{5,13},{6,22},{7,15},{8,24},{9,1... | collective-permute-start | bytes 884744 | tf_op jit(solution)/shard_map/ppermute | solution.py:1348
  83.8 1.9 %collective-permute-start.23 = (bf16[64,2048]{1,0:T(8,128)(2,1)S(1)}, bf16[64,2048]{1,0:T(8,128)(2,1)S(1)}, u32[]{:S(2)}, u32[]{:S(2)}) collective-permute-start(bf16[64,2048]{1,0:T(8,128)(2,1)S(1)} %get-tuple-element.202), channel_id=1, source_target_pairs={{0,1},{1,0},{2,3},{3,2},{4,5},{5,4},{6,7},{7,6},{8,9},{9,8},{10,11... | collective-permute-start | bytes 786440 | tf_op jit(solution)/shard_map/ppermute | solution.py:1326
  83.9 1.9 %collective-permute-start.24 = (bf16[64,2048]{1,0:T(8,128)(2,1)S(1)}, bf16[64,2048]{1,0:T(8,128)(2,1)S(1)}, u32[]{:S(2)}, u32[]{:S(2)}) collective-permute-start(bf16[64,2048]{1,0:T(8,128)(2,1)S(1)} %get-tuple-element.203), channel_id=1, source_target_pairs={{0,1},{1,0},{2,3},{3,2},{4,5},{5,4},{6,7},{7,6},{8,9},{9,8},{10,11... | collective-permute-start | bytes 786440 | tf_op jit(solution)/shard_map/ppermute | solution.py:1326
  84.4 3.9 %collective-permute-start.26 = (f32[16,512]{1,0:T(8,128)S(1)}, f32[16,512]{1,0:T(8,128)S(1)}, u32[]{:S(2)}, u32[]{:S(2)}) collective-permute-start(f32[16,512]{1,0:T(8,128)S(1)} %add.7.sums_ref), channel_id=1, source_target_pairs={{0,16},{1,9},{2,18},{3,11},{4,20},{5,13},{6,22},{7,15},{8,24},{9,1... | collective-permute-start | bytes 98312 | tf_op jit(solution)/shard_map/ppermute | solution.py:1348
where the time goes:
time: 89.3 us; the launch traced here: 89.2 us
  Pallas kernels  57.7 us (65%)
  starting transfers between devices  26.3 us (29%)
  waiting for transfers between devices  3.21 us (4%)
  other arithmetic  1.02 us (1%)
    pallas_call x16, Pallas kernels, call_kernel(): pl.pallas_call(kernel, out_shape=[held[place](*output) for output, place...  57.7 us
    ppermute x17, starting transfers between devices, send_height(): return lax.ppermute(block, 'height', [(i, i ^ step) for i in range(size)])  13.4 us
    ppermute x7, starting transfers between devices, send_phase(): return lax.ppermute(block, ('canvas', 'height'), pairs)  9.32 us
    ppermute x3, starting transfers between devices, send_canvas(): return lax.ppermute(block, 'canvas', [(i, i ^ step) for i in range(size)])  3.55 us
  transfers between devices with their start and end apart: 27, of which 8 were waited for; matrix products, arithmetic and copies ran while one was open for 1% of the time, Pallas kernels for 55%

commit v1 on v0

--- a/solution.py
+++ b/solution.py
@@ -19,7 +19,7 @@
 FILL_ROWS = 256
 QUERY_ROWS = 512
 SCORE_ROWS = 256
-KEY_ROWS = 512
+KEY_ROWS = 256
 
 
 def extended(block, sides, width):
@@ -452,7 +452,7 @@
         value = old_ref[rows, :] + mask * part
         total_ref[rows, :] = value if last is None else last(rows, value)
 
-    block = 2 * FILL_ROWS if last is None else FILL_ROWS
+    block = pixels if last is None else FILL_ROWS
     for start in range(0, pixels, block):
         step(pl.ds(start, block), pl.ds(start + row_tap * cols, block))
 
@@ -879,14 +879,10 @@
         if index + 1 < len(scores_refs):
             score(index + 1)
         soften(index)
-
-    def collect(rows, carry):
-        out_flip_ref[rows, :] = jnp.dot(
-            value_flip_ref[rows, :], soft_ref[...], preferred_element_type=wide
+        rows = slice(index * block, (index + 1) * block)
+        out_flip_ref[:, rows] = jnp.dot(
+            value_flip_ref[...], soft_ref[:, rows], preferred_element_type=wide
         ).astype(jnp.bfloat16)
-        return carry
-
-    each_block(channels, channels // 2, collect)
     height = lax.axis_index("height")
     own = pl.ds(pl.multiple_of(height * own_pixels, own_pixels), own_pixels)
     output_ref[...] = (

time: 89.3 us -> 88.9 us (level)
  no operation moved by 1% of the time
where the time goes in v1:
time: 88.9 us; the launch traced here: 88.8 us
  Pallas kernels  57.3 us (64%)
  starting transfers between devices  26.3 us (30%)
  waiting for transfers between devices  3.2 us (4%)
  other arithmetic  1.02 us (1%)
    pallas_call x16, Pallas kernels, call_kernel(): pl.pallas_call(kernel, out_shape=[held[place](*output) for output, place...  57.3 us
    ppermute x17, starting transfers between devices, send_height(): return lax.ppermute(block, 'height', [(i, i ^ step) for i in range(size)])  13.4 us
    ppermute x7, starting transfers between devices, send_phase(): return lax.ppermute(block, ('canvas', 'height'), pairs)  9.32 us
    ppermute x3, starting transfers between devices, send_canvas(): return lax.ppermute(block, 'canvas', [(i, i ^ step) for i in range(size)])  3.55 us
  transfers between devices with their start and end apart: 27, of which 8 were waited for; matrix products, arithmetic and copies ran while one was open for 1% of the time, Pallas kernels for 55%

profile of v1, /device:TPU:0, one launch (start us, length us, event | category | flops | bytes accessed | tf_op | source)
XLA Modules:
  0.0 88.8 jit_solution(16246366301371365592)
XLA Ops:
  0.6 5.1 %collective-permute-start.5 = (bf16[128,512]{1,0:T(8,128)(2,1)}, bf16[128,512]{1,0:T(8,128)(2,1)S(1)}, u32[]{:S(2)}, u32[]{:S(2)}) collective-permute-start(bf16[128,512]{1,0:T(8,128)(2,1)} %bitcast.8), channel_id=1, source_target_pairs={{0,6},{1,7},{2,4},{3,5},{4,2},{5,3},{6,0},{7,1},{8,14},{9,15},{10,... | collective-permute-start | bytes 393224 | tf_op jit(solution)/shard_map/ppermute | solution.py:1322
  5.8 0.6 collective-permute-start.2
  6.4 1.4 %collective-permute-start.1 = (bf16[128,512]{1,0:T(8,128)(2,1)}, bf16[128,512]{1,0:T(8,128)(2,1)S(1)}, u32[]{:S(2)}, u32[]{:S(2)}) collective-permute-start(bf16[128,512]{1,0:T(8,128)(2,1)} %bitcast.13), channel_id=1, source_target_pairs={{0,2},{1,3},{2,0},{3,1},{4,6},{5,7},{6,4},{7,5},{8,10},{9,11},{10,... | collective-permute-start | bytes 393224 | tf_op jit(solution)/shard_map/ppermute | solution.py:1322
  7.8 1.0 %pad_maximum_fusion = bf16[256,512]{1,0:T(8,128)(2,1)S(1)} fusion(bf16[128,512]{1,0:T(8,128)(2,1)} %bitcast.14, bf16[128,512]{1,0:T(8,128)(2,1)} %bitcast.11), kind=kLoop, calls=%fused_computation | loop fusion | flops 524288 | bytes 524288 | tf_op jit(solution)/shard_map/concatenate | solution.py:1446
  8.9 7.4 %shard_map.186 = (bf16[2,3,3,512,512]{4,3,2,1,0:T(8,128)(2,1)S(1)}, bf16[2,3,512,1536]{3,2,1,0:T(8,128)(2,1)S(1)}, bf16[512,1536]{1,0:T(8,128)(2,1)S(1)}, bf16[5...) custom-call(s32[1,64]{1,0:T(1,128)} %ids_hbm.1, ...), custom_call_target="tpu_custom_call" | custom-call | flops 4831838208 | bytes 301989888 | tf_op jit(solution)/shard_map/pallas_call | solution.py:1308
  16.3 0.9 collective-permute-done.4.refs_4_
  17.2 0.5 collective-permute-start.6
  18.0 3.4 %collective-permute-start.9 = (bf16[128,512]{1,0:T(8,128)(2,1)S(1)}, bf16[128,512]{1,0:T(8,128)(2,1)S(1)}, u32[]{:S(2)}, u32[]{:S(2)}) collective-permute-start(bf16[128,512]{1,0:T(8,128)(2,1)S(1)} %bitcast.16), channel_id=1, source_target_pairs={{0,6},{1,7},{2,4},{3,5},{4,2},{5,3},{6,0},{7,1},{8,14},{9,15},{10,... | collective-permute-start | bytes 393224 | tf_op jit(solution)/shard_map/ppermute | solution.py:1322
  21.4 13.0 %shard_map.187 = (bf16[1024,512]{1,0:T(8,128)(2,1)S(1)}, bf16[1024,512]{1,0:T(8,128)(2,1)S(1)}, f32[1024,512]{1,0:T(8,128)S(1)}, bf16[1024,512]{1,0:T(8,128)(2,1...) custom-call(bf16[128,512]{1,0:T(8,128)(2,1)} %bitcast.12, bf16[256,512]{1,0:T(8,128)(2,1)S(1)} %collective-permute-done.refs_1_, ...), custom_call_target="tpu_custom_call" | custom-call | flops 9663676416 | bytes 603979776 | tf_op jit(solution)/shard_map/pallas_call | solution.py:1308
  35.1 6.1 %shard_map.188 = (bf16[1024,512]{1,0:T(8,128)(2,1)S(1)}, bf16[1024,512]{1,0:T(8,128)(2,1)S(1)}, bf16[1024,512]{1,0:T(8,128)(2,1)S(1)}, bf16[1024,512]{1,0:T(8,12...) custom-call(bf16[512,1536]{1,0:T(8,128)(2,1)S(1)} %get-tuple-element.118.qkv_re, ...), custom_call_target="tpu_custom_call" | custom-call | flops 3758096384 | bytes 234881024 | tf_op jit(solution)/shard_map/pallas_call | solution.py:1308
  41.2 7.5 %shard_map.189 = (bf16[1024,512]{1,0:T(8,128)(2,1)S(1)}, bf16[1024,1536]{1,0:T(8,128)(2,1)S(1)}, f32[16,512]{1,0:T(8,128)S(1)}, bf16[64,2048]{1,0:T(8,128)(2,1)S(1)}, bf16[64,2048]{1,0:T(8,128)(2,1)S(1)}) custom-call(bf16[512,512]{1,0:T(8,128)(2,1)S(1)} %get-tuple-element.119.proj_ref, bf16[1024,512]{1,0:T(8,128)(2,1)S(1)} %get-tuple-element.142.normed_ref, ...), custom_call_target="tpu_custom_call" | custom-call | flops 5905580032 | bytes 369098752 | tf_op jit(solution)/shard_map/pallas_call | solution.py:1308
  48.7 1.6 %collective-permute-start.13 = (bf16[64,2048]{1,0:T(8,128)(2,1)S(1)}, bf16[64,2048]{1,0:T(8,128)(2,1)S(1)}, u32[]{:S(2)}, u32[]{:S(2)}) collective-permute-start(bf16[64,2048]{1,0:T(8,128)(2,1)S(1)} %get-tuple-element.162), channel_id=1, source_target_pairs={{0,8},{1,17},{2,10},{3,19},{4,12},{5,21},{6,14},{7,23},{8,0},{9,25... | collective-permute-start | bytes 786440 | tf_op jit(solution)/shard_map/ppermute | solution.py:1344
  50.2 4.3 %shard_map.190 = (f32[1024,512]{1,0:T(8,128)S(1)}, bf16[1024,512]{1,0:T(8,128)(2,1)S(1)}, f32[16,512]{1,0:T(8,128)S(1)}, bf16[576,512]{1,0:T(8,128)(2,1)S(1)}) custom-call(bf16[512,1536]{1,0:T(8,128)(2,1)S(1)} %get-tuple-element.118.qkv_ref, bf16[1024,512]{1,0:T(8,128)(2,1)S(1)} %get-tuple-element.156.grad_ref, ...), custom_call_target="tpu_custom_call" | custom-call | flops 2214592512 | bytes 138412032 | tf_op jit(solution)/shard_map/pallas_call | solution.py:1308
  54.6 0.6 collective-permute-done.13.got_ref
  55.2 1.6 %collective-permute-start.14 = (bf16[32,2048]{1,0:T(8,128)(2,1)S(1)}, bf16[32,2048]{1,0:T(8,128)(2,1)S(1)}, u32[]{:S(2)}, u32[]{:S(2)}) collective-permute-start(bf16[32,2048]{1,0:T(8,128)(2,1)S(1)} %get-tuple-element.170), channel_id=1, source_target_pairs={{0,16},{1,9},{2,18},{3,11},{4,20},{5,13},{6,22},{7,15},{8,24},{9,1... | collective-permute-start | bytes 393224 | tf_op jit(solution)/shard_map/ppermute | solution.py:1344
  56.8 3.5 %shard_map.192 = (f32[1024,512]{1,0:T(8,128)S(1)}, bf16[1056,1536]{1,0:T(8,128)(2,1)S(1)}) custom-call(bf16[1024,512]{1,0:T(8,128)(2,1)S(1)} %get-tuple-element.167.grad_ref, f32[2,1024,128]{2,1,0:T(8,128)S(1)} %get-tuple-element.128.refs_10_.mask_ref, bf16[2,3,512,1536]{3,2,1,0:T(8,128)(2,1)S(1)} %get-tuple-element.168.weights_ref), custom_call_target="tpu_custom_call" | custom-call | flops 3221225472 | bytes 201326592 | tf_op jit(solution)/shard_map/pallas_call | solution.py:1308
  60.3 2.5 %collective-permute-start.17 = (bf16[32,2048]{1,0:T(8,128)(2,1)S(1)}, bf16[32,2048]{1,0:T(8,128)(2,1)S(1)}, u32[]{:S(2)}, u32[]{:S(2)}) collective-permute-start(bf16[32,2048]{1,0:T(8,128)(2,1)S(1)} %add_convert_fusion.refs_0_), channel_id=1, source_target_pairs={{0,24},{8,16},{16,8},{24,0},{1,25},{9,17},{17,9},{25,1},{2,26},{10... | collective-permute-start | bytes 393224 | tf_op jit(solution)/shard_map/ppermute | solution.py:1334
  62.8 0.6 collective-permute-start.16
  63.4 0.5 collective-permute-start.15
  63.9 4.8 %shard_map.193 = (bf16[1024,512]{1,0:T(8,128)(2,1)S(1)}, f32[16,512]{1,0:T(8,128)S(1)}, bf16[1152,128]{1,0:T(8,128)(2,1)S(1)}, bf16[1152,128]{1,0:T(8,128)(2,1)S...) custom-call(f32[1024,512]{1,0:T(8,128)S(1)} %get-tuple-element.171.old_total_ref, ...), custom_call_target="tpu_custom_call" | custom-call | flops 2415919104 | bytes 150994944 | tf_op jit(solution)/shard_map/pallas_call | solution.py:1308
  69.0 1.1 %collective-permute-start.21 = (bf16[128,2048]{1,0:T(8,128)(2,1)S(1)}, bf16[128,2048]{1,0:T(8,128)(2,1)S(1)}, u32[]{:S(2)}, u32[]{:S(2)}) collective-permute-start(bf16[128,2048]{1,0:T(8,128)(2,1)S(1)} %shard_map.194.refs_0_), channel_id=1, source_target_pairs={{0,2},{1,3},{2,0},{3,1},{4,6},{5,7},{6,4},{7,5},{8,10},{9,11},{10,... | collective-permute-start | bytes 1572872 | tf_op jit(solution)/shard_map/ppermute | solution.py:1322
  70.1 1.4 %collective-permute-start.19 = (bf16[1152,128]{1,0:T(8,128)(2,1)S(1)}, bf16[1152,128]{1,0:T(8,128)(2,1)S(1)}, u32[]{:S(2)}, u32[]{:S(2)}) collective-permute-start(bf16[1152,128]{1,0:T(8,128)(2,1)S(1)} %get-tuple-element.191), channel_id=1, source_target_pairs={{0,8},{1,17},{2,10},{3,19},{4,12},{5,21},{6,14},{7,23},{8,0},{9,25... | collective-permute-start | bytes 884744 | tf_op jit(solution)/shard_map/ppermute | solution.py:1344
  71.5 0.6 collective-permute-start.20
  72.1 5.7 %shard_map.195 = (f32[128,512]{1,0:T(8,128)S(1)}, f32[16,512]{1,0:T(8,128)S(1)}, f32[16,512]{1,0:T(8,128)S(1)}) custom-call(bf16[1024,512]{1,0:T(8,128)(2,1)S(1)} %get-tuple-element.187.grad_one_ref, bf16[1024,512]{1,0:T(8,128)(2,1)S(1)} %get-tuple-element.188.features_ref, f32[24,512]{1,0:T(8,128)S(1)} %get-tuple-element.133.table_ref, ...), custom_call_target="tpu_custom_call" | custom-call | flops 1 | tf_op jit(solution)/shard_map/pallas_call | solution.py:1308
  77.8 1.4 %collective-permute-start.22 = (f32[16,512]{1,0:T(8,128)S(1)}, f32[16,512]{1,0:T(8,128)S(1)}, u32[]{:S(2)}, u32[]{:S(2)}) collective-permute-start(f32[16,512]{1,0:T(8,128)S(1)} %get-tuple-element.190), channel_id=1, source_target_pairs={{0,8},{1,17},{2,10},{3,19},{4,12},{5,21},{6,14},{7,23},{8,0},{9,25... | collective-permute-start | bytes 98312 | tf_op jit(solution)/shard_map/ppermute | solution.py:1344
  79.3 0.7 collective-permute-done.20.got_two_ref
  80.1 1.4 %collective-permute-start.25 = (bf16[1152,128]{1,0:T(8,128)(2,1)S(1)}, bf16[1152,128]{1,0:T(8,128)(2,1)S(1)}, u32[]{:S(2)}, u32[]{:S(2)}) collective-permute-start(bf16[1152,128]{1,0:T(8,128)(2,1)S(1)} %get-tuple-element.211), channel_id=1, source_target_pairs={{0,16},{1,9},{2,18},{3,11},{4,20},{5,13},{6,22},{7,15},{8,24},{9,1... | collective-permute-start | bytes 884744 | tf_op jit(solution)/shard_map/ppermute | solution.py:1344
  81.5 1.4 %shard_map.197 = (f32[512,1536]{1,0:T(8,128)}, f32[512,512]{1,0:T(8,128)}) custom-call(bf16[128,2048]{1,0:T(8,128)(2,1)S(1)} %shard_map.194.refs_0_, bf16[128,2048]{1,0:T(8,128)(2,1)S(1)} %collective-permute-done.18.refs_1_), custom_call_target="tpu_custom_call" | custom-call | flops 1 | tf_op jit(solution)/shard_map/pallas_call | solution.py:1308
  84.0 1.3 %collective-permute-start.26 = (f32[16,512]{1,0:T(8,128)S(1)}, f32[16,512]{1,0:T(8,128)S(1)}, u32[]{:S(2)}, u32[]{:S(2)}) collective-permute-start(f32[16,512]{1,0:T(8,128)S(1)} %add.7.sums_ref), channel_id=1, source_target_pairs={{0,16},{1,9},{2,18},{3,11},{4,20},{5,13},{6,22},{7,15},{8,24},{9,1... | collective-permute-start | bytes 98312 | tf_op jit(solution)/shard_map/ppermute | solution.py:1344
  85.4 1.4 %shard_map.199 = (f32[512,1536]{1,0:T(8,128)}, f32[512,512]{1,0:T(8,128)}) custom-call(bf16[128,2048]{1,0:T(8,128)(2,1)S(1)} %collective-permute-done.21.packed_ref.chip_ref, bf16[64,2048]{1,0:T(8,128)(2,1)S(1)} %collective-permute-done.23.both_a_ref, ...), custom_call_target="tpu_custom_call", output_to_operand_aliasing={{0}: (3, {}), {1}: (4, {})} | custom-call | flops 1 | tf_op jit(solution)/shard_map/pallas_call | solution.py:1308
  86.8 1.1 %shard_map.200 = bf16[128,512]{1,0:T(8,128)(2,1)} custom-call(f32[128,512]{1,0:T(8,128)S(1)} %get-tuple-element.208.own_ref, f32[16,512]{1,0:T(8,128)S(1)} %get-tuple-element.209.partial_ref, bf16[1024,512]{1,0:T(8,128)(2,1)S(1)} %get-tuple-element.188.features_ref, f32[1024,512]{1,0:T(8,128)S(1)} %get-tuple-element.210.residual_grad_ref, ...), custom_call_target="tpu_custom_call" | custom-call | flops 134217728 | bytes 8388608 | tf_op jit(solution)/shard_map/pallas_call | solution.py:1308
  87.9 0.9 shard_map.201
  (43 shorter events, 2.8 us)
Async XLA Ops:
  0.6 15.6 %collective-permute-start.5 = (bf16[128,512]{1,0:T(8,128)(2,1)}, bf16[128,512]{1,0:T(8,128)(2,1)S(1)}, u32[]{:S(2)}, u32[]{:S(2)}) collective-permute-start(bf16[128,512]{1,0:T(8,128)(2,1)} %bitcast.8), channel_id=1, source_target_pairs={{0,6},{1,7},{2,4},{3,5},{4,2},{5,3},{6,0},{7,1},{8,14},{9,15},{10,... | collective-permute-start | bytes 393224 | tf_op jit(solution)/shard_map/ppermute | solution.py:1322
  5.8 11.4 %collective-permute-start.4 = (bf16[128,512]{1,0:T(8,128)(2,1)}, bf16[128,512]{1,0:T(8,128)(2,1)S(1)}, u32[]{:S(2)}, u32[]{:S(2)}) collective-permute-start(bf16[128,512]{1,0:T(8,128)(2,1)} %bitcast.9), channel_id=1, source_target_pairs={{0,4},{1,5},{2,6},{3,7},{4,0},{5,1},{6,2},{7,3},{8,12},{9,13},{10,... | collective-permute-start | bytes 393224 | tf_op jit(solution)/shard_map/ppermute | solution.py:1322
  5.8 11.4 %collective-permute-start.2 = (bf16[128,512]{1,0:T(8,128)(2,1)}, bf16[128,512]{1,0:T(8,128)(2,1)S(1)}, u32[]{:S(2)}, u32[]{:S(2)}) collective-permute-start(bf16[128,512]{1,0:T(8,128)(2,1)} %bitcast.10), channel_id=1, source_target_pairs={{0,2},{1,3},{2,0},{3,1},{4,6},{5,7},{6,4},{7,5},{8,10},{9,11},{10,... | collective-permute-start | bytes 393224 | tf_op jit(solution)/shard_map/ppermute | solution.py:1322
  6.4 11.6 %collective-permute-start.1 = (bf16[128,512]{1,0:T(8,128)(2,1)}, bf16[128,512]{1,0:T(8,128)(2,1)S(1)}, u32[]{:S(2)}, u32[]{:S(2)}) collective-permute-start(bf16[128,512]{1,0:T(8,128)(2,1)} %bitcast.13), channel_id=1, source_target_pairs={{0,2},{1,3},{2,0},{3,1},{4,6},{5,7},{6,4},{7,5},{8,10},{9,11},{10,... | collective-permute-start | bytes 393224 | tf_op jit(solution)/shard_map/ppermute | solution.py:1322
  8.8 12.6 %collective-permute-start = (bf16[256,512]{1,0:T(8,128)(2,1)S(1)}, bf16[256,512]{1,0:T(8,128)(2,1)S(1)}, u32[]{:S(2)}, u32[]{:S(2)}) collective-permute-start(bf16[256,512]{1,0:T(8,128)(2,1)S(1)} %pad_maximum_fusion), channel_id=1, source_target_pairs={{0,1},{1,0},{2,3},{3,2},{4,5},{5,4},{6,7},{7,6},{8,9},{9,8},{10,11... | collective-permute-start | bytes 786440 | tf_op jit(solution)/shard_map/ppermute | solution.py:1322
  8.9 9.1 %copy-start = (bf16[1,8,16,512]{3,2,1,0:T(8,128)(2,1)S(1)}, bf16[1,8,16,512]{3,2,1,0:T(8,128)(2,1)}, u32[]{:S(2)}) copy-start(bf16[1,8,16,512]{3,2,1,0:T(8,128)(2,1)} %param.21) | copy-start | bytes 393220
  17.1 4.2 %collective-permute-start.3 = (bf16[128,512]{1,0:T(8,128)(2,1)S(1)}, bf16[128,512]{1,0:T(8,128)(2,1)S(1)}, u32[]{:S(2)}, u32[]{:S(2)}) collective-permute-start(bf16[128,512]{1,0:T(8,128)(2,1)S(1)} %collective-permute-done.2.refs_2_), channel_id=1, source_target_pairs={{0,1},{1,0},{2,3},{3,2},{4,5},{5,4},{6,7},{7,6},{8,9},{9,8},{10,11... | collective-permute-start | bytes 393224 | tf_op jit(solution)/shard_map/ppermute | solution.py:1322
  17.2 4.2 %collective-permute-start.6 = (bf16[128,512]{1,0:T(8,128)(2,1)S(1)}, bf16[128,512]{1,0:T(8,128)(2,1)S(1)}, u32[]{:S(2)}, u32[]{:S(2)}) collective-permute-start(bf16[128,512]{1,0:T(8,128)(2,1)S(1)} %collective-permute-done.4.refs_4_), channel_id=1, source_target_pairs={{0,1},{1,0},{2,3},{3,2},{4,5},{5,4},{6,7},{7,6},{8,9},{9,8},{10,11... | collective-permute-start | bytes 393224 | tf_op jit(solution)/shard_map/ppermute | solution.py:1322
  17.7 3.7 %collective-permute-start.7 = (bf16[128,512]{1,0:T(8,128)(2,1)S(1)}, bf16[128,512]{1,0:T(8,128)(2,1)S(1)}, u32[]{:S(2)}, u32[]{:S(2)}) collective-permute-start(bf16[128,512]{1,0:T(8,128)(2,1)S(1)} %collective-permute-done.5.refs_6_), channel_id=1, source_target_pairs={{0,1},{1,0},{2,3},{3,2},{4,5},{5,4},{6,7},{7,6},{8,9},{9,8},{10,11... | collective-permute-start | bytes 393224 | tf_op jit(solution)/shard_map/ppermute | solution.py:1322
  18.0 16.4 %collective-permute-start.9 = (bf16[128,512]{1,0:T(8,128)(2,1)S(1)}, bf16[128,512]{1,0:T(8,128)(2,1)S(1)}, u32[]{:S(2)}, u32[]{:S(2)}) collective-permute-start(bf16[128,512]{1,0:T(8,128)(2,1)S(1)} %bitcast.16), channel_id=1, source_target_pairs={{0,6},{1,7},{2,4},{3,5},{4,2},{5,3},{6,0},{7,1},{8,14},{9,15},{10,... | collective-permute-start | bytes 393224 | tf_op jit(solution)/shard_map/ppermute | solution.py:1322
  21.4 13.1 %collective-permute-start.8 = (bf16[128,512]{1,0:T(8,128)(2,1)S(1)}, bf16[128,512]{1,0:T(8,128)(2,1)S(1)}, u32[]{:S(2)}, u32[]{:S(2)}) collective-permute-start(bf16[128,512]{1,0:T(8,128)(2,1)S(1)} %bitcast.17), channel_id=1, source_target_pairs={{0,4},{1,5},{2,6},{3,7},{4,0},{5,1},{6,2},{7,3},{8,12},{9,13},{10,... | collective-permute-start | bytes 393224 | tf_op jit(solution)/shard_map/ppermute | solution.py:1322
  34.4 6.7 %collective-permute-start.10 = (bf16[128,512]{1,0:T(8,128)(2,1)S(1)}, bf16[128,512]{1,0:T(8,128)(2,1)S(1)}, u32[]{:S(2)}, u32[]{:S(2)}) collective-permute-start(bf16[128,512]{1,0:T(8,128)(2,1)S(1)} %collective-permute-done.1.refs_2_), channel_id=1, source_target_pairs={{0,1},{1,0},{2,3},{3,2},{4,5},{5,4},{6,7},{7,6},{8,9},{9,8},{10,11... | collective-permute-start | bytes 393224 | tf_op jit(solution)/shard_map/ppermute | solution.py:1322
  34.5 6.6 %collective-permute-start.11 = (bf16[128,512]{1,0:T(8,128)(2,1)S(1)}, bf16[128,512]{1,0:T(8,128)(2,1)S(1)}, u32[]{:S(2)}, u32[]{:S(2)}) collective-permute-start(bf16[128,512]{1,0:T(8,128)(2,1)S(1)} %collective-permute-done.8.refs_4_), channel_id=1, source_target_pairs={{0,1},{1,0},{2,3},{3,2},{4,5},{5,4},{6,7},{7,6},{8,9},{9,8},{10,11... | collective-permute-start | bytes 393224 | tf_op jit(solution)/shard_map/ppermute | solution.py:1322
  35.0 6.2 %collective-permute-start.12 = (bf16[128,512]{1,0:T(8,128)(2,1)S(1)}, bf16[128,512]{1,0:T(8,128)(2,1)S(1)}, u32[]{:S(2)}, u32[]{:S(2)}) collective-permute-start(bf16[128,512]{1,0:T(8,128)(2,1)S(1)} %collective-permute-done.9.refs_6_), channel_id=1, source_target_pairs={{0,1},{1,0},{2,3},{3,2},{4,5},{5,4},{6,7},{7,6},{8,9},{9,8},{10,11... | collective-permute-start | bytes 393224 | tf_op jit(solution)/shard_map/ppermute | solution.py:1322
  48.7 6.4 %collective-permute-start.13 = (bf16[64,2048]{1,0:T(8,128)(2,1)S(1)}, bf16[64,2048]{1,0:T(8,128)(2,1)S(1)}, u32[]{:S(2)}, u32[]{:S(2)}) collective-permute-start(bf16[64,2048]{1,0:T(8,128)(2,1)S(1)} %get-tuple-element.162), channel_id=1, source_target_pairs={{0,8},{1,17},{2,10},{3,19},{4,12},{5,21},{6,14},{7,23},{8,0},{9,25... | collective-permute-start | bytes 786440 | tf_op jit(solution)/shard_map/ppermute | solution.py:1344
  55.2 5.1 %collective-permute-start.14 = (bf16[32,2048]{1,0:T(8,128)(2,1)S(1)}, bf16[32,2048]{1,0:T(8,128)(2,1)S(1)}, u32[]{:S(2)}, u32[]{:S(2)}) collective-permute-start(bf16[32,2048]{1,0:T(8,128)(2,1)S(1)} %get-tuple-element.170), channel_id=1, source_target_pairs={{0,16},{1,9},{2,18},{3,11},{4,20},{5,13},{6,22},{7,15},{8,24},{9,1... | collective-permute-start | bytes 393224 | tf_op jit(solution)/shard_map/ppermute | solution.py:1344
  60.3 8.4 %collective-permute-start.17 = (bf16[32,2048]{1,0:T(8,128)(2,1)S(1)}, bf16[32,2048]{1,0:T(8,128)(2,1)S(1)}, u32[]{:S(2)}, u32[]{:S(2)}) collective-permute-start(bf16[32,2048]{1,0:T(8,128)(2,1)S(1)} %add_convert_fusion.refs_0_), channel_id=1, source_target_pairs={{0,24},{8,16},{16,8},{24,0},{1,25},{9,17},{17,9},{25,1},{2,26},{10... | collective-permute-start | bytes 393224 | tf_op jit(solution)/shard_map/ppermute | solution.py:1334
  62.8 6.1 %collective-permute-start.16 = (bf16[32,2048]{1,0:T(8,128)(2,1)S(1)}, bf16[32,2048]{1,0:T(8,128)(2,1)S(1)}, u32[]{:S(2)}, u32[]{:S(2)}) collective-permute-start(bf16[32,2048]{1,0:T(8,128)(2,1)S(1)} %add_convert_fusion.refs_0_), channel_id=1, source_target_pairs={{0,16},{8,24},{16,0},{24,8},{1,17},{9,25},{17,1},{25,9},{2,18},{10... | collective-permute-start | bytes 393224 | tf_op jit(solution)/shard_map/ppermute | solution.py:1334
  63.4 5.5 %collective-permute-start.15 = (bf16[32,2048]{1,0:T(8,128)(2,1)S(1)}, bf16[32,2048]{1,0:T(8,128)(2,1)S(1)}, u32[]{:S(2)}, u32[]{:S(2)}) collective-permute-start(bf16[32,2048]{1,0:T(8,128)(2,1)S(1)} %add_convert_fusion.refs_0_), channel_id=1, source_target_pairs={{0,8},{8,0},{16,24},{24,16},{1,9},{9,1},{17,25},{25,17},{2,10},{10... | collective-permute-start | bytes 393224 | tf_op jit(solution)/shard_map/ppermute | solution.py:1334
  68.9 11.0 %collective-permute-start.18 = (bf16[128,2048]{1,0:T(8,128)(2,1)S(1)}, bf16[128,2048]{1,0:T(8,128)(2,1)S(1)}, u32[]{:S(2)}, u32[]{:S(2)}) collective-permute-start(bf16[128,2048]{1,0:T(8,128)(2,1)S(1)} %shard_map.194.refs_0_), channel_id=1, source_target_pairs={{0,1},{1,0},{2,3},{3,2},{4,5},{5,4},{6,7},{7,6},{8,9},{9,8},{10,11... | collective-permute-start | bytes 1572872 | tf_op jit(solution)/shard_map/ppermute | solution.py:1322
  69.0 14.3 %collective-permute-start.21 = (bf16[128,2048]{1,0:T(8,128)(2,1)S(1)}, bf16[128,2048]{1,0:T(8,128)(2,1)S(1)}, u32[]{:S(2)}, u32[]{:S(2)}) collective-permute-start(bf16[128,2048]{1,0:T(8,128)(2,1)S(1)} %shard_map.194.refs_0_), channel_id=1, source_target_pairs={{0,2},{1,3},{2,0},{3,1},{4,6},{5,7},{6,4},{7,5},{8,10},{9,11},{10,... | collective-permute-start | bytes 1572872 | tf_op jit(solution)/shard_map/ppermute | solution.py:1322
  70.1 9.2 %collective-permute-start.19 = (bf16[1152,128]{1,0:T(8,128)(2,1)S(1)}, bf16[1152,128]{1,0:T(8,128)(2,1)S(1)}, u32[]{:S(2)}, u32[]{:S(2)}) collective-permute-start(bf16[1152,128]{1,0:T(8,128)(2,1)S(1)} %get-tuple-element.191), channel_id=1, source_target_pairs={{0,8},{1,17},{2,10},{3,19},{4,12},{5,21},{6,14},{7,23},{8,0},{9,25... | collective-permute-start | bytes 884744 | tf_op jit(solution)/shard_map/ppermute | solution.py:1344
  71.5 8.5 %collective-permute-start.20 = (bf16[1152,128]{1,0:T(8,128)(2,1)S(1)}, bf16[1152,128]{1,0:T(8,128)(2,1)S(1)}, u32[]{:S(2)}, u32[]{:S(2)}) collective-permute-start(bf16[1152,128]{1,0:T(8,128)(2,1)S(1)} %get-tuple-element.192), channel_id=1, source_target_pairs={{0,8},{1,17},{2,10},{3,19},{4,12},{5,21},{6,14},{7,23},{8,0},{9,25... | collective-permute-start | bytes 884744 | tf_op jit(solution)/shard_map/ppermute | solution.py:1344
  77.8 5.1 %collective-permute-start.22 = (f32[16,512]{1,0:T(8,128)S(1)}, f32[16,512]{1,0:T(8,128)S(1)}, u32[]{:S(2)}, u32[]{:S(2)}) collective-permute-start(f32[16,512]{1,0:T(8,128)S(1)} %get-tuple-element.190), channel_id=1, source_target_pairs={{0,8},{1,17},{2,10},{3,19},{4,12},{5,21},{6,14},{7,23},{8,0},{9,25... | collective-permute-start | bytes 98312 | tf_op jit(solution)/shard_map/ppermute | solution.py:1344
  80.1 7.8 %collective-permute-start.25 = (bf16[1152,128]{1,0:T(8,128)(2,1)S(1)}, bf16[1152,128]{1,0:T(8,128)(2,1)S(1)}, u32[]{:S(2)}, u32[]{:S(2)}) collective-permute-start(bf16[1152,128]{1,0:T(8,128)(2,1)S(1)} %get-tuple-element.211), channel_id=1, source_target_pairs={{0,16},{1,9},{2,18},{3,11},{4,20},{5,13},{6,22},{7,15},{8,24},{9,1... | collective-permute-start | bytes 884744 | tf_op jit(solution)/shard_map/ppermute | solution.py:1344
  83.4 1.9 %collective-permute-start.23 = (bf16[64,2048]{1,0:T(8,128)(2,1)S(1)}, bf16[64,2048]{1,0:T(8,128)(2,1)S(1)}, u32[]{:S(2)}, u32[]{:S(2)}) collective-permute-start(bf16[64,2048]{1,0:T(8,128)(2,1)S(1)} %get-tuple-element.202), channel_id=1, source_target_pairs={{0,1},{1,0},{2,3},{3,2},{4,5},{5,4},{6,7},{7,6},{8,9},{9,8},{10,11... | collective-permute-start | bytes 786440 | tf_op jit(solution)/shard_map/ppermute | solution.py:1322
  83.5 1.9 %collective-permute-start.24 = (bf16[64,2048]{1,0:T(8,128)(2,1)S(1)}, bf16[64,2048]{1,0:T(8,128)(2,1)S(1)}, u32[]{:S(2)}, u32[]{:S(2)}) collective-permute-start(bf16[64,2048]{1,0:T(8,128)(2,1)S(1)} %get-tuple-element.203), channel_id=1, source_target_pairs={{0,1},{1,0},{2,3},{3,2},{4,5},{5,4},{6,7},{7,6},{8,9},{9,8},{10,11... | collective-permute-start | bytes 786440 | tf_op jit(solution)/shard_map/ppermute | solution.py:1322
  84.0 3.9 %collective-permute-start.26 = (f32[16,512]{1,0:T(8,128)S(1)}, f32[16,512]{1,0:T(8,128)S(1)}, u32[]{:S(2)}, u32[]{:S(2)}) collective-permute-start(f32[16,512]{1,0:T(8,128)S(1)} %add.7.sums_ref), channel_id=1, source_target_pairs={{0,16},{1,9},{2,18},{3,11},{4,20},{5,13},{6,22},{7,15},{8,24},{9,1... | collective-permute-start | bytes 98312 | tf_op jit(solution)/shard_map/ppermute | solution.py:1344
